TPU v7x, 256 devices: a whole 4x4x8 slice. The times are simulated.
256 devices in a mesh: wide: 32 (over x_lo, z, core), narrow: 8 (over y, x_hi).
Axes of the slice: x: 4 (x_hi: 2, x_lo: 2; x = x_hi * 2 + x_lo), y: 4, z: 8, core: 2. Of those that a mesh axis runs over, the one named last changes fastest.
Arguments:
- activations: bfloat16 [256, 256, 32, 256], P('wide', 'narrow'), may hold values from -6 to 6
- cotangent: bfloat16 [256, 256, 32, 256], P('wide', 'narrow'), may hold values from -6 to 6
- point_weight: bfloat16 [32, 32], replicated, may hold values from -1 to 1
- bias: float32 [32], replicated, may hold values from -3 to 3
- spectral_weight: bfloat16 [2, 32, 32, 16, 32, 32], P(None, 'wide', 'narrow'), may hold values from -6 to 6
Outputs:
- input_grad: bfloat16 [256, 256, 32, 256], P('wide', 'narrow')
- point_grad: float32 [32, 32], replicated
- bias_grad: float32 [32], replicated
- spectral_grad: float32 [2, 32, 32, 16, 32, 32], P(None, 'wide', 'narrow')
All inputs are finite; a program needn't handle non-finite values.
Results may differ from a plain program's by a relative error of at most 0.0065.
Values sent between devices are 32-bit elements; how exact they have to be, the bound alone decides.
A program may use at most 128 MiB of HBM per device.

v0:
```python
import math

import jax
import jax.numpy as jnp
from jax import lax
from jax.sharding import PartitionSpec as P

M = 16


def contract(form, left, right):
    return jnp.einsum(
        form, left, right, precision=lax.Precision.HIGH, preferred_element_type=jnp.float32
    )


def precise_product(form, left, right):
    return jnp.einsum(
        form, left, right, precision=lax.Precision.HIGHEST, preferred_element_type=jnp.float32
    )


def kept_freq(index, length, half):
    return jnp.where(index < half, index, length - 2 * half + index)


def phase_tables(freqs, cells, length):
    product = freqs[:, None] * cells[None, :] % length
    angle = product.astype(jnp.float32) * (2.0 * math.pi / length)
    return (jnp.cos(angle), jnp.sin(angle))


def rotate(real_part, imag_part, cosine, sine, sign_value, form):
    first = contract(form, real_part, cosine) - sign_value * contract(form, imag_part, sine)
    second = contract(form, imag_part, cosine) + sign_value * contract(form, real_part, sine)
    return (first, second)


def depth_forward(field, modes):
    length = field.shape[3]
    cosine, sine = phase_tables(
        jnp.arange(modes, dtype=jnp.int32), jnp.arange(length, dtype=jnp.int32), length
    )
    real_part = contract("abcz,kz->abck", field, cosine)
    imag_part = -contract("abcz,kz->abck", field, sine)
    shape = (field.shape[0], field.shape[1], -1)
    return (real_part.reshape(shape), imag_part.reshape(shape))


def depth_inverse(real_part, imag_part, depth_weights, length):
    modes = depth_weights.shape[0]
    shape = (real_part.shape[0], real_part.shape[1], real_part.shape[2] // modes, modes)
    cosine, sine = phase_tables(
        jnp.arange(modes, dtype=jnp.int32), jnp.arange(length, dtype=jnp.int32), length
    )
    return contract(
        "abck,kz->abcz", real_part.reshape(shape), cosine * depth_weights[:, None]
    ) - contract("abck,kz->abcz", imag_part.reshape(shape), sine * depth_weights[:, None])


def mix_modes(coeffs, weight):
    lead_x, lead_y = (coeffs.shape[0], coeffs.shape[1])
    modes = weight.shape[3]
    split = coeffs.reshape(lead_x, lead_y, 2, -1, modes)
    factor = weight.astype(jnp.float32)
    real_part = precise_product("pqck,pqkco->pqok", split[:, :, 0], factor[0]) - precise_product(
        "pqck,pqkco->pqok", split[:, :, 1], factor[1]
    )
    imag_part = precise_product("pqck,pqkco->pqok", split[:, :, 0], factor[1]) + precise_product(
        "pqck,pqkco->pqok", split[:, :, 1], factor[0]
    )
    return jnp.stack((real_part, imag_part), axis=2).reshape(lead_x, lead_y, 2, -1)


def weight_terms(coeffs, grads, weight):
    lead_x, lead_y = (coeffs.shape[0], coeffs.shape[1])
    modes = weight.shape[3]
    split_c = coeffs.reshape(lead_x, lead_y, 2, -1, modes)
    split_g = grads.reshape(lead_x, lead_y, 2, -1, modes)
    form = "pqck,pqok->pqkco"
    grad_real = precise_product(form, split_c[:, :, 0], split_g[:, :, 0]) + precise_product(
        form, split_c[:, :, 1], split_g[:, :, 1]
    )
    grad_imag = precise_product(form, split_c[:, :, 0], split_g[:, :, 1]) - precise_product(
        form, split_c[:, :, 1], split_g[:, :, 0]
    )
    factor = weight.astype(jnp.float32)
    back = "pqok,pqkco->pqck"
    back_real = precise_product(back, split_g[:, :, 0], factor[0]) + precise_product(
        back, split_g[:, :, 1], factor[1]
    )
    back_imag = precise_product(back, split_g[:, :, 1], factor[0]) - precise_product(
        back, split_g[:, :, 0], factor[1]
    )
    coeff_grad = jnp.stack((back_real, back_imag), axis=2).reshape(lead_x, lead_y, 2, -1)
    return (jnp.stack((grad_real, grad_imag), axis=0), coeff_grad)


def local(activations, cotangent, point_weight, bias, spectral_weight):
    size_x = lax.axis_size("wide")
    size_y = lax.axis_size("narrow")
    rows_x, rows_y, channels, length = activations.shape
    span_x = rows_x * size_x
    span_y = rows_y * size_y
    scale = 1.0 / math.sqrt(span_x * span_y * length)
    local_x = 2 * M // size_x
    local_y = 2 * M // size_y
    features = channels * M
    cells_x = lax.axis_index("wide") * rows_x + jnp.arange(rows_x, dtype=jnp.int32)
    cells_y = lax.axis_index("narrow") * rows_y + jnp.arange(rows_y, dtype=jnp.int32)
    all_modes = jnp.arange(2 * M, dtype=jnp.int32)
    depth_weights = jnp.where(jnp.arange(M, dtype=jnp.int32) == 0, 1.0, 2.0).astype(jnp.float32)
    unit_weights = jnp.ones((M,), jnp.float32)

    def to_modes(field):
        real_part, imag_part = depth_forward(field, M)
        cos_y, sin_y = phase_tables(kept_freq(all_modes, span_y, M), cells_y, span_y)
        cos_x, sin_x = phase_tables(kept_freq(all_modes, span_x, M), cells_x, span_x)
        re_y, im_y = rotate(real_part, imag_part, cos_y, sin_y, -1.0, "ayf,ky->kaf")
        re_x, im_x = rotate(re_y, im_y, cos_x, sin_x, -1.0, "qaf,ka->kqf")
        full = jnp.stack((re_x, im_x), axis=2)
        blocked = (
            full.reshape(size_x, local_x, size_y, local_y, 2, features)
            .transpose(0, 2, 1, 3, 4, 5)
            .reshape(4 * M * M, 2, features)
        )
        result = lax.psum_scatter(
            blocked, ("wide", "narrow"), scatter_dimension=0, tiled=True
        ).reshape(local_x, local_y, 2, features)
        return result * scale

    def to_field(modes, weights_here):
        whole = lax.all_gather(
            modes.reshape(local_x * local_y, 2, features), ("wide", "narrow"), axis=0, tiled=True
        )
        ordered = (
            whole.reshape(size_x, size_y, local_x, local_y, 2, features)
            .transpose(0, 2, 1, 3, 4, 5)
            .reshape(2 * M, 2 * M, 2, features)
        )
        cos_x, sin_x = phase_tables(kept_freq(all_modes, span_x, M), cells_x, span_x)
        cos_y, sin_y = phase_tables(kept_freq(all_modes, span_y, M), cells_y, span_y)
        re_x, im_x = rotate(ordered[:, :, 0], ordered[:, :, 1], cos_x, sin_x, 1.0, "kqf,ka->aqf")
        real_part, imag_part = rotate(re_x, im_x, cos_y, sin_y, 1.0, "akf,ky->ayf")
        return depth_inverse(real_part, imag_part, weights_here, length) * scale

    coeffs = to_modes(activations)
    mixed = mix_modes(coeffs, spectral_weight)
    spectral = to_field(mixed, depth_weights)
    point = jnp.einsum(
        "abcz,co->aboz", activations, point_weight, preferred_element_type=jnp.float32
    )
    preact = spectral + point + bias[None, None, :, None]
    _, pullback = jax.vjp(jax.nn.gelu, preact)
    pre_grad = pullback(cotangent.astype(jnp.float32))[0].astype(jnp.bfloat16)
    grad_modes = to_modes(pre_grad)
    grads = (grad_modes.reshape(local_x, local_y, 2, channels, M) * depth_weights).reshape(
        local_x, local_y, 2, features
    )
    spectral_grad, coeff_grad = weight_terms(coeffs, grads, spectral_weight)
    back = to_field(coeff_grad, unit_weights)
    mixing_back = jnp.einsum(
        "aboz,co->abcz", pre_grad, point_weight, preferred_element_type=jnp.float32
    )
    input_grad = (mixing_back + back).astype(jnp.bfloat16)
    weight_sum = jnp.einsum(
        "abcz,aboz->co", activations, pre_grad, preferred_element_type=jnp.float32
    )
    bias_sum = jnp.sum(pre_grad.astype(jnp.float32), axis=(0, 1, 3))
    point_total, bias_total = lax.psum((weight_sum, bias_sum), ("wide", "narrow"))
    return (input_grad, point_total * scale, bias_total * scale, spectral_grad)


def solution(mesh):
    return jax.shard_map(
        local,
        mesh=mesh,
        in_specs=(
            P("wide", "narrow", None, None),
            P("wide", "narrow", None, None),
            P(),
            P(),
            P(None, "wide", "narrow", None, None, None),
        ),
        out_specs=(
            P("wide", "narrow", None, None),
            P(),
            P(),
            P(None, "wide", "narrow", None, None, None),
        ),
        check_vma=False,
    )
```

profile of v0, /device:TPU:1, one launch (start us, length us, event | category | flops | bytes accessed | tf_op | source)
XLA Modules:
  0.0 2122.2 jit_solution(8341795437255912561)
XLA Ops:
  7.2 9.2 negate_bitcast_fusion
  16.4 6.9 convolution_bitcast_fusion
  23.3 2.6 copy.102
  25.9 3.6 copy.99
  42.6 2.5 pad_maximum_fusion
  45.1 270.8 %all-reduce.6.cloned.1.call-done = f32[1024,2,512]{2,0,1:T(8,128)} async-done(((f32[1024,2,512]{2,0,1:T(8,128)}), f32[1024,2,512]{2,0,1:T(8,128)}) %all-reduce.6.cloned.1.call-update) | async-done | bytes 4194320
  319.7 6.7 fusion.101
  326.4 700.8 %all-gather.3.cloned.1.call-done = f32[1024,2,512]{2,1,0:T(2,128)} async-done(((f32[4,2,512]{2,1,0:T(2,128)}), f32[1024,2,512]{2,1,0:T(2,128)}) %all-gather.3.cloned.1.call-update) | async-done | bytes 4194320 | tf_op jit(solution)/shard_map/all_gather | solution.py:133
  1027.1 3.0 copy.117
  1034.4 1.8 fusion.24
  1041.1 2.0 fusion.29
  1044.7 2.4 copy.123
  1048.7 2.4 copy.127
  1051.0 5.2 fusion.69
  1056.3 13.2 convert_reduce_fusion
  1069.5 6.9 convolution_negate_fusion
  1076.4 5.6 fusion.12
  1082.0 3.7 copy.132
  1085.7 2.9 convolution_multiply_fusion.1
  1100.3 2.4 pad_maximum_fusion.1
  1102.8 266.2 %all-reduce.8.cloned.1.call-done = f32[1024,2,512]{2,0,1:T(8,128)} async-done(((f32[1024,2,512]{2,0,1:T(8,128)}), f32[1024,2,512]{2,0,1:T(8,128)}) %all-reduce.8.cloned.1.call-update) | async-done | bytes 4194320
  1372.5 4.7 convolution_bitcast_fusion.1
  1377.1 78.3 %all-reduce.2 = (f32[32,32]{0,1:T(8,128)S(1)}, f32[32]{0:T(128)S(1)}) all-reduce(f32[32,32]{0,1:T(8,128)S(1)} %convolution_bitcast_fusion.1, f32[32]{0:T(128)S(1)} %get-tuple-element.40), channel_id=1, replica_groups=mesh['wide'=32,'narrow'=8] {'wide','narrow'}, use_global_device_ids=true, to_apply=%region_2.3 | all-reduce | flops 1056 | bytes 8448 | tf_op jit(solution)/shard_map/psum | solution.py:170
  1456.7 6.7 fusion.99
  1465.5 614.9 %all-gather.5.cloned.1.call-done = f32[1024,2,512]{2,1,0:T(2,128)} async-done(((f32[4,2,512]{2,1,0:T(2,128)}), f32[1024,2,512]{2,1,0:T(2,128)}) %all-gather.5.cloned.1.call-update) | async-done | bytes 4194320 | tf_op jit(solution)/shard_map/all_gather | solution.py:133
  2080.4 3.0 copy.147
  2094.5 1.9 copy.152
  2096.4 2.6 copy.153
  2099.1 1.9 copy.156
  2101.0 3.4 copy.157
  2104.4 3.5 fusion.74
  2107.9 7.6 fusion.10
  (108 shorter events, 58.7 us)
Async XLA Ops:
  7.2 312.5 %copy-start = (bf16[32,32]{1,0:T(8,128)(2,1)S(1)}, bf16[32,32]{1,0:T(8,128)(2,1)}, u32[]{:S(2)}) copy-start(bf16[32,32]{1,0:T(8,128)(2,1)} %param.7) | copy-start | bytes 6148
  7.2 308.7 %all-reduce.6.cloned.1.call-start = ((), (), s32[]{:S(2)}) async-start(), calls=%async_computation.2 | async-start | bytes 8388608
  7.2 9.2 copy-start.1
  29.5 1.6 copy-start.4
  45.0 271.9 %copy-start.6 = (bf16[2,1,4,16,32,32]{5,4,3,2,1,0:T(8,128)(2,1)S(1)}, bf16[2,1,4,16,32,32]{5,4,3,2,1,0:T(8,128)(2,1)}, u32[]{:S(2)}) copy-start(bf16[2,1,4,16,32,32]{5,4,3,2,1,0:T(8,128)(2,1)} %param.9) | copy-start | bytes 786436
  45.0 982.1 %all-gather.3.cloned.1.call-start = ((), (), s32[]{:S(2)}) async-start(), calls=%async_computation | async-start | bytes 4210688 | tf_op jit(solution)/shard_map/all_gather | solution.py:133
  319.4 1049.6 %all-reduce.8.cloned.1.call-start = ((), (), s32[]{:S(2)}) async-start(), calls=%async_computation.3 | async-start | bytes 8388608
  1051.0 5.2 copy-start.7
  1051.0 5.3 copy-start.8
  1051.0 5.3 copy-start.9
  1069.5 6.9 copy-start.2
  1090.0 1.6 copy-start.3
  1102.7 977.7 %all-gather.5.cloned.1.call-start = ((), (), s32[]{:S(2)}) async-start(), calls=%async_computation.1 | async-start | bytes 4210688 | tf_op jit(solution)/shard_map/all_gather | solution.py:133
  2104.4 3.5 copy-start.5
Sparse Core Ops, SparseCore 0:
  45.2 270.6 all-reduce.5
  319.5 707.5 all-gather.2
  1102.9 266.1 all-reduce.7
  1372.6 707.8 all-gather.4
where the time goes:
time: 2130 us; the launch traced here: 2120 us
  waiting for transfers between devices  1850 us (87%)
  matrix products  120 us (6%)
  blocking collectives  78.3 us (4%)
  local copies, waits for them, and re-layouts  44.2 us (2%)
    all_gather x2, waiting for transfers between devices, to_field(): lax.all_gather(modes.reshape(local_x * local_y, 2, features), ('wide', 'n...  1320 us
    unnamed x6, waiting for transfers between devices  537 us
    dot_general x40, matrix products, contract(): jnp.einsum(form, left, right, precision=lax.Precision.HIGH, preferred_ele...  102 us
    psum x1, blocking collectives, local(): lax.psum((weight_sum, bias_sum), ('wide', 'narrow'))  78.3 us
  transfers between devices with their start and end apart: 4, of which 4 were waited for; matrix products, arithmetic and copies ran while one was open for 1% of the time, Pallas kernels for 0%

commit v1 on v0

v1 whole, which is shorter than its diff:
```python
import functools
import math

import jax
import jax.numpy as jnp
import ml_dtypes
import numpy as np
from jax import lax
from jax.experimental import pallas as pl
from jax.experimental.pallas import tpu as pltpu
from jax.sharding import PartitionSpec as P

WIDE = 32
NARROW = 8
M = 16
C = 32
NZ = 256
XL = 8
YL = 32
KY = 4
SCALE = 1.0 / 4096.0

F32 = jnp.float32
BF16 = jnp.bfloat16


def kept(j):
    return np.where(j < 16, j, 224 + j)


def trig(freqs, cells):
    angle = (np.outer(freqs, cells) % 256) * (2.0 * math.pi / 256.0)
    return np.cos(angle), np.sin(angle)


def split_np(table):
    hi = table.astype(np.float32).astype(ml_dtypes.bfloat16)
    lo = (table - hi.astype(np.float64)).astype(np.float32).astype(ml_dtypes.bfloat16)
    return hi, lo


@functools.lru_cache(maxsize=None)
def tables():
    freqs = kept(np.arange(32))
    cos_a, sin_a = trig(freqs, np.arange(256))
    cos_z, sin_z = trig(np.arange(M), np.arange(NZ))
    eye_x = np.eye(XL)
    cy = cos_a.reshape(NARROW, KY, NARROW, YL)
    sy = sin_a.reshape(NARROW, KY, NARROW, YL)
    both = np.stack((cy, sy))
    yf = np.einsum("dtkny,xu->ntkxudy", both, eye_x).reshape(NARROW, 256, 512)
    both = np.stack((cy, -sy))
    yi = np.einsum("dtkny,xu->nxydktu", both, eye_x).reshape(NARROW, 256, 512)
    xf = np.concatenate((cos_a, sin_a), axis=1) * SCALE
    xi = np.concatenate((cos_a.T, -sin_a.T), axis=1)
    zf = np.tile(np.concatenate((cos_z, -sin_z), axis=0).T, (1, 4))
    depth = np.where(np.arange(M) == 0, 1.0, 2.0)[:, None]

    def inverse_z(weights):
        one = np.concatenate((cos_z * weights, -sin_z * weights), axis=0) * SCALE
        full = np.zeros((4, 128, NZ))
        for g in range(4):
            full[g, g * 32 : (g + 1) * 32] = one
        hi, lo = split_np(full)
        return np.concatenate((hi, hi, lo), axis=1)

    return dict(
        yf=np.stack(split_np(yf), axis=1),
        yi=np.stack(split_np(yi), axis=1),
        xf=np.stack(split_np(xf)),
        xi=np.stack(split_np(xi)),
        zf=np.concatenate(split_np(zf), axis=1),
        ziw=inverse_z(depth),
        zi1=inverse_z(np.ones((M, 1))),
    )


def dot(a, b):
    return jnp.dot(a, b, preferred_element_type=F32)


def halves(x):
    hi = x.astype(BF16)
    return hi, (x - hi.astype(F32)).astype(BF16)


def dot3(table, index, hi, lo):
    t_hi = table[index, 0] if index is not None else table[0]
    t_lo = table[index, 1] if index is not None else table[1]
    return dot(t_hi, hi) + (dot(t_hi, lo) + dot(t_lo, hi))


def turn(x):
    lane = lax.broadcasted_iota(jnp.int32, x.shape, x.ndim - 1)
    real = lax.rem(lane, 32) < 16
    return jnp.where(real, pltpu.roll(x, 112, x.ndim - 1), -pltpu.roll(x, 16, x.ndim - 1))


def remote(src, dst, send, recv, device):
    return pltpu.make_async_remote_copy(
        src_ref=src,
        dst_ref=dst,
        send_sem=send,
        recv_sem=recv,
        device_id=device,
        device_id_type=pl.DeviceIdType.MESH,
    )


def greet(n, w):
    barrier = pltpu.get_barrier_semaphore()

    def one(axis, me, size):
        def body(k, carry):
            pl.semaphore_signal(
                barrier,
                inc=1,
                device_id={axis: lax.rem(me + k, size)},
                device_id_type=pl.DeviceIdType.MESH,
            )
            return carry

        lax.fori_loop(1, size, body, 0)

    one("narrow", n, NARROW)
    one("wide", w, WIDE)
    return barrier


def greeted(barrier):
    pl.semaphore_wait(barrier, NARROW + WIDE - 2)


def others(me, size, fn):
    def body(k, carry):
        fn(lax.rem(me + k, size))
        return carry

    lax.fori_loop(1, size, body, 0)


def depth_forward(field, zf):
    full = dot(field.reshape(YL * C, NZ), zf)
    full = (full[:, :128] + full[:, 128:]).reshape(YL, 4, 8, 128)
    lane = lax.broadcasted_iota(jnp.int32, (YL, 8, 128), 2)
    low = jnp.where(lane < 32, full[:, 0], full[:, 1])
    high = jnp.where(lane < 96, full[:, 2], full[:, 3])
    return jnp.where(lane < 64, low, high)


def put_rows(x, depth, d_ref, rh_ref, rl_ref):
    d_ref[...] = depth.reshape(YL * 8, 128)
    rows = pl.multiple_of(x * 64, 64)
    for c8 in range(8):
        part = d_ref[pl.ds(c8, YL, stride=8), :]
        lanes = slice((c8 % 2) * 128, (c8 % 2) * 128 + 128)
        hi, lo = halves(part)
        rh_ref[c8 // 2, pl.ds(rows, 32), lanes] = hi
        rl_ref[c8 // 2, pl.ds(rows, 32), lanes] = lo
        hi, lo = halves(turn(part))
        rows_t = pl.multiple_of(rows + 32, 32)
        rh_ref[c8 // 2, pl.ds(rows_t, 32), lanes] = hi
        rl_ref[c8 // 2, pl.ds(rows_t, 32), lanes] = lo


class Forward:
    scratch = dict(
        d=pltpu.VMEM((256, 128), F32),
        rh=pltpu.VMEM((4, 512, 256), BF16),
        rl=pltpu.VMEM((4, 512, 256), BF16),
        ys=pltpu.VMEM((4, NARROW, 32, 256), F32),
        yr=pltpu.VMEM((4, NARROW, 32, 256), F32),
        xs=pltpu.VMEM((WIDE, 8, 128), F32),
        xr=pltpu.VMEM((WIDE, 8, 128), F32),
        ms=pltpu.VMEM((WIDE, 1, 128), F32),
        mr=pltpu.VMEM((WIDE, 1, 128), F32),
        y_send=pltpu.SemaphoreType.DMA((4, NARROW)),
        y_recv=pltpu.SemaphoreType.DMA((4, NARROW)),
        x_send=pltpu.SemaphoreType.DMA((WIDE,)),
        x_recv=pltpu.SemaphoreType.DMA((WIDE,)),
        m_send=pltpu.SemaphoreType.DMA((WIDE,)),
        m_recv=pltpu.SemaphoreType.DMA((WIDE,)),
    )

    @staticmethod
    def run(s, n, w, yf_ref, xf_ref):
        def send_y(q, carry):
            out = dot3(yf_ref, None, s.rh[q], s.rl[q])
            s.ys[q] = out.reshape(NARROW, 32, 256)
            s.yr[q, n] = s.ys[q, n]
            others(
                n,
                NARROW,
                lambda t: remote(
                    s.ys.at[q, t], s.yr.at[q, n], s.y_send.at[q, t], s.y_recv.at[q, n], {"narrow": t}
                ).start(),
            )
            return carry

        lax.fori_loop(0, 4, send_y, 0)

        def sum_y(q, carry):
            others(
                n,
                NARROW,
                lambda t: remote(
                    s.ys.at[q, t], s.yr.at[q, t], s.y_send.at[q, t], s.y_recv.at[q, t], {"narrow": t}
                ).wait_recv(),
            )
            total = s.yr[q, 0]
            for t in range(1, NARROW):
                total = total + s.yr[q, t]
            for k in range(KY):
                for j in range(2):
                    to = k * 8 + 2 * q + j
                    tile = total[k * 8 : k * 8 + 8, j * 128 : j * 128 + 128]
                    s.xs[to] = tile

                    @pl.when(to == w)
                    def _():
                        s.xr[w] = s.xs[to]

                    @pl.when(to != w)
                    def _():
                        remote(
                            s.xs.at[to], s.xr.at[w], s.x_send.at[to], s.x_recv.at[w], {"wide": to}
                        ).start()

            return carry

        lax.fori_loop(0, 4, sum_y, 0)
        others(
            w,
            WIDE,
            lambda t: remote(
                s.xs.at[t], s.xr.at[t], s.x_send.at[t], s.x_recv.at[t], {"wide": t}
            ).wait_recv(),
        )
        cells = s.xr[...].reshape(256, 128)
        hi, lo = halves(jnp.concatenate((cells, turn(cells)), axis=0))
        modes = dot3(xf_ref, None, hi, lo)
        s.ms[...] = modes.reshape(WIDE, 1, 128)
        s.mr[w] = s.ms[w]
        others(
            w,
            WIDE,
            lambda t: remote(
                s.ms.at[t], s.mr.at[w], s.m_send.at[t], s.m_recv.at[w], {"wide": t}
            ).start(),
        )
        others(
            w,
            WIDE,
            lambda t: remote(
                s.ms.at[t], s.mr.at[t], s.m_send.at[t], s.m_recv.at[t], {"wide": t}
            ).wait_recv(),
        )

    @staticmethod
    def finish(s, n, w):
        def per_q(q, carry):
            others(
                n,
                NARROW,
                lambda t: remote(
                    s.ys.at[q, t], s.yr.at[q, t], s.y_send.at[q, t], s.y_recv.at[q, t], {"narrow": t}
                ).wait_send(),
            )
            return carry

        lax.fori_loop(0, 4, per_q, 0)

        def per_t(t):
            remote(
                s.xs.at[t], s.xr.at[t], s.x_send.at[t], s.x_recv.at[t], {"wide": t}
            ).wait_send()
            remote(
                s.ms.at[t], s.mr.at[t], s.m_send.at[t], s.m_recv.at[t], {"wide": t}
            ).wait_send()

        others(w, WIDE, per_t)


class Inverse:
    scratch = dict(
        nr=pltpu.VMEM((WIDE, 1, 128), F32),
        vs=pltpu.VMEM((WIDE, 8, 128), F32),
        vr=pltpu.VMEM((KY, 8, 8, 128), F32),
        ag=pltpu.VMEM((KY, NARROW, 8, 8, 128), F32),
        s=pltpu.VMEM((XL * 256, 128), F32),
        n_send=pltpu.SemaphoreType.DMA((WIDE,)),
        n_recv=pltpu.SemaphoreType.DMA((WIDE,)),
        v_send=pltpu.SemaphoreType.DMA((WIDE,)),
        v_recv=pltpu.SemaphoreType.DMA((WIDE,)),
        a_send=pltpu.SemaphoreType.DMA((KY, NARROW)),
        a_recv=pltpu.SemaphoreType.DMA((KY, NARROW)),
    )

    @staticmethod
    def start(s, n, w, modes_ref):
        s.nr[w] = modes_ref[w]
        others(
            w,
            WIDE,
            lambda t: remote(
                modes_ref.at[t], s.nr.at[w], s.n_send.at[t], s.n_recv.at[w], {"wide": t}
            ).start(),
        )

    @staticmethod
    def run(s, n, w, modes_ref, yi_ref, xi_ref):
        others(
            w,
            WIDE,
            lambda t: remote(
                modes_ref.at[t], s.nr.at[t], s.n_send.at[t], s.n_recv.at[t], {"wide": t}
            ).wait_recv(),
        )
        modes = s.nr[...].reshape(WIDE, 128)
        hi, lo = halves(jnp.concatenate((modes, turn(modes)), axis=0))
        cells = dot3(xi_ref, None, hi, lo)
        s.vs[...] = cells.reshape(WIDE, 8, 128)
        own_k, own_c = w // 8, lax.rem(w, 8)
        s.vr[own_k, own_c] = s.vs[w]
        others(
            w,
            WIDE,
            lambda t: remote(
                s.vs.at[t], s.vr.at[own_k, own_c], s.v_send.at[t], s.v_recv.at[w], {"wide": t}
            ).start(),
        )

        def per_k(k, carry):
            def arrived(c, inner):
                t = k * 8 + c

                @pl.when(t != w)
                def _():
                    remote(
                        s.vs.at[t], s.vr.at[k, c], s.v_send.at[t], s.v_recv.at[t], {"wide": t}
                    ).wait_recv()

                return inner

            lax.fori_loop(0, 8, arrived, 0)
            s.ag[k, n] = s.vr[k]
            others(
                n,
                NARROW,
                lambda t: remote(
                    s.vr.at[k], s.ag.at[k, n], s.a_send.at[k, t], s.a_recv.at[k, n], {"narrow": t}
                ).start(),
            )
            return carry

        lax.fori_loop(0, KY, per_k, 0)

    @staticmethod
    def to_depth(s, n, yi_ref):
        def wait_k(k, carry):
            others(
                n,
                NARROW,
                lambda t: remote(
                    s.vr.at[k], s.ag.at[k, t], s.a_send.at[k, t], s.a_recv.at[k, t], {"narrow": t}
                ).wait_recv(),
            )
            return carry

        lax.fori_loop(0, KY, wait_k, 0)

        def pair(p, carry):
            columns = []
            for j in range(2):
                part = s.ag[:, :, 2 * p + j].reshape(256, 128)
                columns.append(jnp.concatenate((part, turn(part)), axis=0))
            hi, lo = halves(jnp.concatenate(columns, axis=1))
            out = dot3(yi_ref, None, hi, lo)
            for x in range(XL):
                for j in range(2):
                    s.s[pl.ds(x * 256 + 2 * p + j, YL, stride=8), :] = out[
                        x * YL : x * YL + YL, j * 128 : j * 128 + 128
                    ]
            return carry

        lax.fori_loop(0, 4, pair, 0)

    @staticmethod
    def depth_inverse(s, x, zi_ref, field_ref):
        rows = pl.multiple_of(x * 256, 256)
        hi, lo = halves(s.s[pl.ds(rows, 256), :])
        both = jnp.concatenate((hi, lo, hi), axis=1)
        for g in range(4):
            field_ref[:, g] = dot(both, zi_ref[g]).reshape(YL, 8, NZ)

    @staticmethod
    def finish(s, n, w, modes_ref):
        def per_t(t):
            remote(
                modes_ref.at[t], s.nr.at[t], s.n_send.at[t], s.n_recv.at[t], {"wide": t}
            ).wait_send()
            remote(
                s.vs.at[t], s.vr.at[0, 0], s.v_send.at[t], s.v_recv.at[t], {"wide": t}
            ).wait_send()

        others(w, WIDE, per_t)

        def per_k(k, carry):
            others(
                n,
                NARROW,
                lambda t: remote(
                    s.vr.at[k], s.ag.at[k, t], s.a_send.at[k, t], s.a_recv.at[k, t], {"narrow": t}
                ).wait_send(),
            )
            return carry

        lax.fori_loop(0, KY, per_k, 0)


class Names:
    def __init__(self, names, refs):
        for name, ref in zip(names, refs):
            setattr(self, name, ref)


def each_x(fn):
    def body(x, carry):
        fn(x)
        return carry

    lax.fori_loop(0, XL, body, 0)


def forward_kernel(names, act_hbm, yf_hbm, xf_ref, zf_ref, out_ref, *refs):
    s = Names(names, refs)
    n, w = lax.axis_index("narrow"), lax.axis_index("wide")
    each_x(lambda x: pltpu.make_async_copy(act_hbm.at[x], s.act.at[x], s.act_sem.at[x]).start())
    table = pltpu.make_async_copy(yf_hbm.at[n], s.yf, s.table_sem.at[0])
    table.start()
    barrier = greet(n, w)

    def step(x):
        pltpu.make_async_copy(act_hbm.at[x], s.act.at[x], s.act_sem.at[x]).wait()
        put_rows(x, depth_forward(s.act[x], zf_ref[...]), s.d, s.rh, s.rl)

    each_x(step)
    table.wait()
    greeted(barrier)
    Forward.run(s, n, w, s.yf, xf_ref)
    out_ref[...] = s.mr[...]
    Forward.finish(s, n, w)


def fold_point(full):
    row = lax.broadcasted_iota(jnp.int32, full.shape, 0) // 32
    lane = lax.broadcasted_iota(jnp.int32, full.shape, 1) // 32
    full = jnp.where(row == lane, full, 0.0)
    total = full[0:32]
    for y in range(1, 8):
        total = total + full[y * 32 : y * 32 + 32]
    total = total[:, :128] + total[:, 128:]
    total = total + pltpu.roll(total, 64, 1)
    total = total + pltpu.roll(total, 32, 1)
    lane = lax.broadcasted_iota(jnp.int32, (8, 128), 1)
    low = jnp.where(lane < 32, total[0:8], total[8:16])
    high = jnp.where(lane < 96, total[16:24], total[24:32])
    return jnp.where(lane < 64, low, high)


def gelu_slope(u):
    k = math.sqrt(2.0 / math.pi)
    square = u * u
    t = jnp.tanh(k * (u + 0.044715 * (square * u)))
    inner = k * (1.0 + (3 * 0.044715) * square)
    return 0.5 * (1.0 + t) + 0.5 * u * ((1.0 - t * t) * inner)


def middle_kernel(
    names,
    modes_ref,
    act_hbm,
    cot_hbm,
    yf_hbm,
    yi_hbm,
    xf_ref,
    xi_ref,
    zf_ref,
    zi_ref,
    mix_ref,
    bias_ref,
    grads_ref,
    sums_ref,
    pre_hbm,
    *refs,
):
    s = Names(names, refs)
    n, w = lax.axis_index("narrow"), lax.axis_index("wide")
    barrier = greet(n, w)
    tables_in = [
        pltpu.make_async_copy(yi_hbm.at[n], s.yi, s.table_sem.at[0]),
        pltpu.make_async_copy(yf_hbm.at[n], s.yf, s.table_sem.at[1]),
    ]
    for copy in tables_in:
        copy.start()

    def fetch(x):
        pltpu.make_async_copy(act_hbm.at[x], s.act.at[x], s.act_sem.at[x]).start()
        pltpu.make_async_copy(cot_hbm.at[x], s.cot.at[x], s.cot_sem.at[x]).start()

    each_x(fetch)
    greeted(barrier)
    Inverse.start(s, n, w, modes_ref)
    s.pg[...] = jnp.zeros_like(s.pg)
    s.bs[...] = jnp.zeros_like(s.bs)
    for copy in tables_in:
        copy.wait()
    Inverse.run(s, n, w, modes_ref, s.yi, xi_ref)
    Inverse.to_depth(s, n, s.yi)

    def step(x):
        pltpu.make_async_copy(act_hbm.at[x], s.act.at[x], s.act_sem.at[x]).wait()
        pltpu.make_async_copy(cot_hbm.at[x], s.cot.at[x], s.cot_sem.at[x]).wait()
        Inverse.depth_inverse(s, x, zi_ref, s.field)

        def block(b, carry):
            ys = pl.ds(pl.multiple_of(b * 8, 8), 8)
            act = s.act[x, ys].reshape(256, NZ)
            point = dot(mix_ref[...], act)
            preact = s.field[ys].reshape(256, NZ) + point + bias_ref[...]
            slope = gelu_slope(preact)
            pre = (s.cot[x, ys].reshape(256, NZ).astype(F32) * slope).astype(BF16)
            s.pre[x, ys] = pre.reshape(8, C, NZ)
            s.pg[...] += lax.dot_general(
                act, pre, (((1,), (1,)), ((), ())), preferred_element_type=F32
            )
            return carry

        lax.fori_loop(0, 4, block, 0)
        pltpu.make_async_copy(s.pre.at[x], pre_hbm.at[x], s.pre_sem.at[x]).start()
        depth = depth_forward(s.pre[x], zf_ref[...])
        s.bs[...] += jnp.sum(depth, axis=0)
        put_rows(x, depth, s.d, s.rh, s.rl)

    each_x(step)
    s.ps[0:8] = fold_point(s.pg[...])
    s.ps[8:16] = s.bs[...]
    s.pr[n] = s.ps[...]
    Forward.run(s, n, w, s.yf, xf_ref)

    def sum_copy(t, at):
        return remote(s.ps, s.pr.at[at], s.p_send.at[t], s.p_recv.at[at], {"narrow": t})

    others(n, NARROW, lambda t: sum_copy(t, n).start())
    grads_ref[...] = s.mr[...]
    others(n, NARROW, lambda t: sum_copy(t, t).wait_recv())
    total = s.pr[0]
    for t in range(1, NARROW):
        total = total + s.pr[t]
    sums_ref[...] = total
    others(n, NARROW, lambda t: sum_copy(t, t).wait_send())
    each_x(lambda x: pltpu.make_async_copy(s.pre.at[x], pre_hbm.at[x], s.pre_sem.at[x]).wait())
    Inverse.finish(s, n, w, modes_ref)
    Forward.finish(s, n, w)


def last_kernel(
    names,
    modes_ref,
    sums_ref,
    pre_hbm,
    yi_hbm,
    xi_ref,
    zi_ref,
    mix_ref,
    out_hbm,
    total_ref,
    *refs,
):
    s = Names(names, refs)
    n, w = lax.axis_index("narrow"), lax.axis_index("wide")
    barrier = greet(n, w)
    table = pltpu.make_async_copy(yi_hbm.at[n], s.yi, s.table_sem.at[0])
    table.start()
    each_x(lambda x: pltpu.make_async_copy(pre_hbm.at[x], s.pre.at[x], s.pre_sem.at[x]).start())
    greeted(barrier)
    Inverse.start(s, n, w, modes_ref)
    table.wait()
    Inverse.run(s, n, w, modes_ref, s.yi, xi_ref)

    def sum_copy(t, at):
        return remote(sums_ref, s.pr.at[at], s.p_send.at[t], s.p_recv.at[at], {"wide": t})

    s.pr[w] = sums_ref[...]
    others(w, WIDE, lambda t: sum_copy(t, w).start())
    Inverse.to_depth(s, n, s.yi)

    def step(x):
        pltpu.make_async_copy(pre_hbm.at[x], s.pre.at[x], s.pre_sem.at[x]).wait()
        Inverse.depth_inverse(s, x, zi_ref, s.field)

        def block(b, carry):
            ys = pl.ds(pl.multiple_of(b * 8, 8), 8)
            point = dot(mix_ref[...], s.pre[x, ys].reshape(256, NZ))
            out = s.field[ys].reshape(256, NZ) + point
            s.out[x, ys] = out.astype(BF16).reshape(8, C, NZ)
            return carry

        lax.fori_loop(0, 4, block, 0)
        pltpu.make_async_copy(s.out.at[x], out_hbm.at[x], s.out_sem.at[x]).start()

    each_x(step)
    others(w, WIDE, lambda t: sum_copy(t, t).wait_recv())
    total = s.pr[0]
    for t in range(1, WIDE):
        total = total + s.pr[t]
    total_ref[...] = total
    others(w, WIDE, lambda t: sum_copy(t, t).wait_send())
    Inverse.finish(s, n, w, modes_ref)
    each_x(lambda x: pltpu.make_async_copy(s.out.at[x], out_hbm.at[x], s.out_sem.at[x]).wait())


VM = pl.BlockSpec(memory_space=pltpu.VMEM)
HB = pl.BlockSpec(memory_space=pl.ANY)


def call(kernel, name, cid, scratch, in_specs, out_specs, out_shape, *operands):
    return pl.pallas_call(
        functools.partial(kernel, tuple(scratch)),
        name=name,
        in_specs=in_specs,
        out_specs=out_specs,
        out_shape=out_shape,
        scratch_shapes=tuple(scratch.values()),
        compiler_params=pltpu.CompilerParams(
            collective_id=cid, has_side_effects=True, vmem_limit_bytes=56 * 1024 * 1024
        ),
    )(*operands)


FIELD = (XL, YL, C, NZ)


def forward_call(act, tabs):
    scratch = dict(
        Forward.scratch,
        act=pltpu.VMEM(FIELD, BF16),
        yf=pltpu.VMEM((2, 256, 512), BF16),
        act_sem=pltpu.SemaphoreType.DMA((XL,)),
        table_sem=pltpu.SemaphoreType.DMA((2,)),
    )
    return call(
        forward_kernel,
        "field_to_modes",
        0,
        scratch,
        [HB, HB, VM, VM],
        VM,
        jax.ShapeDtypeStruct((WIDE, 1, 128), F32),
        act,
        tabs["yf"],
        tabs["xf"],
        tabs["zf"],
    )


def middle_call(modes, act, cot, mix, bias, tabs):
    scratch = dict(
        Forward.scratch,
        **Inverse.scratch,
        act=pltpu.VMEM(FIELD, BF16),
        cot=pltpu.VMEM(FIELD, BF16),
        pre=pltpu.VMEM(FIELD, BF16),
        field=pltpu.VMEM((YL, 4, 8, NZ), F32),
        yf=pltpu.VMEM((2, 256, 512), BF16),
        yi=pltpu.VMEM((2, 256, 512), BF16),
        pg=pltpu.VMEM((256, 256), F32),
        bs=pltpu.VMEM((8, 128), F32),
        ps=pltpu.VMEM((16, 128), F32),
        pr=pltpu.VMEM((NARROW, 16, 128), F32),
        act_sem=pltpu.SemaphoreType.DMA((XL,)),
        cot_sem=pltpu.SemaphoreType.DMA((XL,)),
        pre_sem=pltpu.SemaphoreType.DMA((XL,)),
        table_sem=pltpu.SemaphoreType.DMA((2,)),
        p_send=pltpu.SemaphoreType.DMA((NARROW,)),
        p_recv=pltpu.SemaphoreType.DMA((NARROW,)),
    )
    return call(
        middle_kernel,
        "modes_to_gradient_modes",
        1,
        scratch,
        [VM, HB, HB, HB, HB, VM, VM, VM, VM, VM, VM],
        [VM, VM, HB],
        [
            jax.ShapeDtypeStruct((WIDE, 1, 128), F32),
            jax.ShapeDtypeStruct((16, 128), F32),
            jax.ShapeDtypeStruct(FIELD, BF16),
        ],
        modes,
        act,
        cot,
        tabs["yf"],
        tabs["yi"],
        tabs["xf"],
        tabs["xi"],
        tabs["zf"],
        tabs["ziw"],
        mix,
        bias,
    )


def last_call(modes, sums, pre, mix, tabs):
    scratch = dict(
        Inverse.scratch,
        pre=pltpu.VMEM(FIELD, BF16),
        out=pltpu.VMEM(FIELD, BF16),
        field=pltpu.VMEM((YL, 4, 8, NZ), F32),
        yi=pltpu.VMEM((2, 256, 512), BF16),
        pr=pltpu.VMEM((WIDE, 16, 128), F32),
        pre_sem=pltpu.SemaphoreType.DMA((XL,)),
        out_sem=pltpu.SemaphoreType.DMA((XL,)),
        table_sem=pltpu.SemaphoreType.DMA((2,)),
        p_send=pltpu.SemaphoreType.DMA((WIDE,)),
        p_recv=pltpu.SemaphoreType.DMA((WIDE,)),
    )
    return call(
        last_kernel,
        "modes_to_input_gradient",
        2,
        scratch,
        [VM, VM, HB, HB, VM, VM, VM],
        [HB, VM],
        [jax.ShapeDtypeStruct(FIELD, BF16), jax.ShapeDtypeStruct((16, 128), F32)],
        modes,
        sums,
        pre,
        tabs["yi"],
        tabs["xi"],
        tabs["zi1"],
        mix,
    )


def precise(form, left, right):
    return jnp.einsum(form, left, right, precision=lax.Precision.HIGHEST, preferred_element_type=F32)


def modes_in(rows):
    return rows.reshape(KY, 8, 4, 2, M).transpose(3, 0, 4, 2, 1).reshape(2, KY, M, C)


def modes_out(parts):
    return (
        parts.reshape(2, KY, M, 4, 8).transpose(1, 4, 3, 0, 2).reshape(WIDE, 1, 128)
    )


def local(activations, cotangent, point_weight, bias, spectral_weight):
    tabs = {name: jnp.asarray(value) for name, value in tables().items()}
    eye = jnp.eye(8, dtype=BF16)
    mix = jnp.kron(eye, point_weight.T)
    mix_back = jnp.kron(eye, point_weight)
    bias_rows = jnp.tile(bias, 8)[:, None]
    weight = spectral_weight[:, 0].astype(F32)

    coeffs = modes_in(forward_call(activations, tabs))
    ahead = "qkc,qkco->qko"
    mixed = jnp.stack(
        (
            precise(ahead, coeffs[0], weight[0]) - precise(ahead, coeffs[1], weight[1]),
            precise(ahead, coeffs[0], weight[1]) + precise(ahead, coeffs[1], weight[0]),
        )
    )
    grad_rows, sums, pre = middle_call(
        modes_out(mixed), activations, cotangent, mix, bias_rows, tabs
    )
    depth_weights = jnp.where(jnp.arange(M, dtype=jnp.int32) == 0, 1.0, 2.0).astype(F32)
    grads = modes_in(grad_rows) * depth_weights[None, None, :, None]
    cr, ci = coeffs[0][..., :, None], coeffs[1][..., :, None]
    gr, gi = grads[0][..., None, :], grads[1][..., None, :]
    spectral_grad = jnp.stack((cr * gr + ci * gi, cr * gi - ci * gr))[:, None]
    back = "qko,qkco->qkc"
    coeff_grad = jnp.stack(
        (
            precise(back, grads[0], weight[0]) + precise(back, grads[1], weight[1]),
            precise(back, grads[1], weight[0]) - precise(back, grads[0], weight[1]),
        )
    )
    input_grad, total = last_call(modes_out(coeff_grad), sums, pre, mix_back, tabs)
    point_grad = total[0:8].reshape(8, 4, C).transpose(1, 0, 2).reshape(C, C) * SCALE
    bias_grad = total[8:16].reshape(8, 4, 2, M)[:, :, 0, 0].T.reshape(C) * SCALE
    return (input_grad, point_grad, bias_grad, spectral_grad)


def solution(mesh):
    return jax.shard_map(
        local,
        mesh=mesh,
        in_specs=(
            P("wide", "narrow", None, None),
            P("wide", "narrow", None, None),
            P(),
            P(),
            P(None, "wide", "narrow", None, None, None),
        ),
        out_specs=(
            P("wide", "narrow", None, None),
            P(),
            P(),
            P(None, "wide", "narrow", None, None, None),
        ),
        check_vma=False,
    )
```

time: 2130 us -> 204 us (0.10)
  waiting for transfers between devices: 1850 us -> 0 us
  Pallas kernels: 0 us -> 182 us
  matrix products: 120 us -> 0 us
  blocking collectives: 78.3 us -> 0 us
  local copies, waits for them, and re-layouts: 44.2 us -> 12.3 us
    all_gather x2 -> x0, waiting for transfers between devices: 1320 us -> none  [to_field(): lax.all_gather(modes.reshape(local_x * local_y, 2, features), ('wide', 'n...]
    unnamed x6 -> x0, waiting for transfers between devices: 537 us -> none
    pallas_call x0 -> x3, Pallas kernels: none -> 182 us  [call(): pl.pallas_call(functools.partial(kernel, tuple(scratch)), name=name, in_s...]
    dot_general x43 -> x0, matrix products: 120 us -> none  [the longest x40 102 us: contract(): jnp.einsum(form, left, right, precision=lax.Precision.HIGH, preferred_ele...]
    psum x1 -> x0, blocking collectives: 78.3 us -> none  [local(): lax.psum((weight_sum, bias_sum), ('wide', 'narrow'))]
  transfers between devices with their start and end apart: 4 -> 0, of which waited for: 4 -> 0; matrix products, arithmetic and copies ran while one was open for 1% -> 0% of each run, Pallas kernels for 0% -> 0%
where the time goes in v1:
time: 204 us; the launch traced here: 203 us
  Pallas kernels  182 us (89%)
  local copies, waits for them, and re-layouts  12.3 us (6%)
  other arithmetic  8.34 us (4%)
    pallas_call x3, Pallas kernels, call(): pl.pallas_call(functools.partial(kernel, tuple(scratch)), name=name, in_s...  182 us

profile of v1, /device:TPU:1, one launch (start us, length us, event | category | flops | bytes accessed | tf_op | source)
XLA Modules:
  0.0 203.2 jit_solution(5830304677269748469)
XLA Ops:
  0.7 0.7 tile.2
  1.3 0.8 copy.21
  2.1 40.9 %field_to_modes.1 = f32[32,1,128]{2,1,0:T(1,128)} custom-call(bf16[8,32,32,256]{3,2,1,0:T(8,128)(2,1)} %act_hbm.3, bf16[8,2,256,512]{3,2,1,0:T(8,128)(2,1)} %constant.10.clone.yf_hbm, bf16[2,32,512]{2,1,0:T(8,128)(2,1)} %constant.25.clone.xf_ref, bf16[256,256]{1,0:T(8,128)(2,1)} %constant.27.clone.zf_ref), custom_call_target="tpu_custom_call" | custom-call | tf_op jit(solution)/shard_map/field_to_modes/pallas_call | solution.py:628
  43.0 0.5 broadcast.106
  43.5 1.4 reduce.22
  44.9 0.2 reshape.105
  45.4 0.8 broadcast_in_dim_tile.4.bias_ref
  46.2 1.2 fusion.2
  47.5 0.1 copy.45
  47.6 0.1 copy.35
  47.8 0.1 copy.20
  47.9 0.8 reshape.106.modes_ref
  48.7 0.1 broadcast_multiply_fusion
  48.8 1.0 mul.159.mix_ref
  49.8 1.0 mul.154.mix_ref
  50.9 92.0 %modes_to_gradient_modes.1 = (f32[32,1,128]{2,1,0:T(1,128)}, f32[16,128]{1,0:T(8,128)}, bf16[8,32,32,256]{3,2,1,0:T(8,128)(2,1)}) custom-call(f32[32,1,128]{2,1,0:T(1,128)} %reshape.106.modes_ref, bf16[8,32,32,256]{3,2,1,0:T(8,128)(2,1)} %act_hbm.3, bf16[8,32,32,256]{3,2,1,0:T(8,128)(2,1)} %cot_hbm.1, bf16[8,2,256,512]{3,2,1,0:T(8,128)(2,1)} %constant.10.clone.yf_hbm, ...), custom_call_target="tpu_custom_call" | custom-call | tf_op jit(solution)/shard_map/modes_to_gradient_modes/pallas_call | solution.py:628
  142.9 1.4 reduce.23
  144.3 0.2 reshape.107
  144.7 1.2 fusion.6
  146.0 0.1 copy.74
  146.3 0.1 copy.24
  146.4 0.8 reshape.109.modes_ref
  147.2 48.8 %modes_to_input_gradient.1 = (bf16[8,32,32,256]{3,2,1,0:T(8,128)(2,1)}, f32[16,128]{1,0:T(8,128)}) custom-call(f32[32,1,128]{2,1,0:T(1,128)} %reshape.109.modes_ref, f32[16,128]{1,0:T(8,128)} %get-tuple-element.10.sums_ref, bf16[8,32,32,256]{3,2,1,0:T(8,128)(2,1)} %get-tuple-element.11.pre_hbm, bf16[8,2,256,512]{3,2,1,0:T(8,128)(2,1)} %constant.24.clone.yi_hbm, ...), custom_call_target="tpu_custom_call" | custom-call | tf_op jit(solution)/shard_map/modes_to_input_gradient/pallas_call | solution.py:628
  196.0 0.7 fusion.9
  196.8 0.6 copy.88
  197.4 0.1 reshape.110
  197.5 0.1 copy.75
  197.6 0.6 mul.169
  198.2 0.6 multiply_add_fusion
  198.8 1.6 maximum_bitcast_fusion
  200.4 0.7 copy-done.1
  201.1 2.0 copy.90
  (28 shorter events, 1.0 us)
Async XLA Ops:
  2.1 44.1 %copy-start = (bf16[2,1,4,16,32,32]{5,4,3,2,1,0:T(8,128)(2,1)S(1)}, bf16[2,1,4,16,32,32]{5,4,3,2,1,0:T(8,128)(2,1)}, u32[]{:S(2)}) copy-start(bf16[2,1,4,16,32,32]{5,4,3,2,1,0:T(8,128)(2,1)} %param.16) | copy-start | bytes 786436
  2.1 46.6 %copy-start.2 = (bf16[32,32]{1,0:T(8,128)(2,1)S(1)}, bf16[32,32]{1,0:T(8,128)(2,1)}, u32[]{:S(2)}) copy-start(bf16[32,32]{1,0:T(8,128)(2,1)} %param.14) | copy-start | bytes 6148
  198.2 2.9 %copy-start.1 = (bf16[8,32,32,256]{3,2,1,0:T(8,128)(2,1)S(1)}, bf16[8,32,32,256]{3,2,1,0:T(8,128)(2,1)}, u32[]{:S(2)}) copy-start(bf16[8,32,32,256]{3,2,1,0:T(8,128)(2,1)} %get-tuple-element.42) | copy-start | bytes 12582916

commit v2 on v0

v2 whole, which is shorter than its diff:
```python
import functools
import math

import jax
import jax.numpy as jnp
import ml_dtypes
import numpy as np
from jax import lax
from jax.experimental import pallas as pl
from jax.experimental.pallas import tpu as pltpu
from jax.sharding import PartitionSpec as P

WIDE = 32
NARROW = 8
M = 16
C = 32
NZ = 256
XL = 8
YL = 32
KY = 4
XC = 2
CHUNKS = XL // XC
ROWS = KY * XC
SCALE = 1.0 / 4096.0

F32 = jnp.float32
BF16 = jnp.bfloat16


def kept(j):
    return np.where(j < 16, j, 224 + j)


def trig(freqs, cells):
    angle = (np.outer(freqs, cells) % 256) * (2.0 * math.pi / 256.0)
    return np.cos(angle), np.sin(angle)


def split_np(table):
    hi = table.astype(np.float32).astype(ml_dtypes.bfloat16)
    lo = (table - hi.astype(np.float64)).astype(np.float32).astype(ml_dtypes.bfloat16)
    return hi, lo


@functools.lru_cache(maxsize=None)
def tables():
    freqs = kept(np.arange(32))
    cos_a, sin_a = trig(freqs, np.arange(256))
    cos_z, sin_z = trig(np.arange(M), np.arange(NZ))
    eye_x = np.eye(XC)
    cy = cos_a.reshape(NARROW, KY, NARROW, YL)
    sy = sin_a.reshape(NARROW, KY, NARROW, YL)
    both = np.stack((cy, sy))
    yf = np.einsum("dtkny,xu->ntkxudy", both, eye_x).reshape(NARROW, 32 * XC, 64 * XC)
    both = np.stack((cy, -sy))
    yi = np.einsum("dtkny,xu->nxydtku", both, eye_x).reshape(NARROW, 32 * XC, 64 * XC)
    xf = np.concatenate((cos_a, sin_a), axis=1) * SCALE
    xi = np.concatenate((cos_a.T, -sin_a.T), axis=1)
    zf = np.tile(np.concatenate((cos_z, -sin_z), axis=0).T, (1, 4))
    depth = np.where(np.arange(M) == 0, 1.0, 2.0)[:, None]

    def inverse_z(weights):
        one = np.concatenate((cos_z * weights, -sin_z * weights), axis=0) * SCALE
        full = np.zeros((4, 128, NZ))
        for g in range(4):
            full[g, g * 32 : (g + 1) * 32] = one
        hi, lo = split_np(full)
        return np.concatenate((hi, hi, lo), axis=1)

    return dict(
        yf=np.stack(split_np(yf), axis=1),
        yi=np.stack(split_np(yi), axis=1),
        xf=np.stack(split_np(xf)),
        xi=np.stack(split_np(xi)),
        zf=np.concatenate(split_np(zf), axis=1),
        ziw=inverse_z(depth),
        zi1=inverse_z(np.ones((M, 1))),
    )


def dot(a, b):
    return jnp.dot(a, b, preferred_element_type=F32)


def dot_t(a, b):
    return lax.dot_general(a, b, (((1,), (1,)), ((), ())), preferred_element_type=F32)


def halves(x):
    hi = x.astype(BF16)
    return hi, (x - hi.astype(F32)).astype(BF16)


def dot3(table, hi, lo):
    t_hi, t_lo = table[0], table[1]
    return dot(t_hi, hi) + (dot(t_hi, lo) + dot(t_lo, hi))


def lane_of(shape):
    return lax.broadcasted_iota(jnp.int32, shape, len(shape) - 1)


def turn(x):
    real = lax.rem(lane_of(x.shape), 32) < 16
    return jnp.where(real, pltpu.roll(x, 112, x.ndim - 1), -pltpu.roll(x, 16, x.ndim - 1))


def remote(src, dst, send, recv, device):
    return pltpu.make_async_remote_copy(
        src_ref=src,
        dst_ref=dst,
        send_sem=send,
        recv_sem=recv,
        device_id=device,
        device_id_type=pl.DeviceIdType.MESH,
    )


def others(me, size, fn):
    def body(k, carry):
        fn(lax.rem(me + k, size))
        return carry

    lax.fori_loop(1, size, body, 0)


def greet(n, w):
    barrier = pltpu.get_barrier_semaphore()

    def signal(axis):
        return lambda t: pl.semaphore_signal(
            barrier, inc=1, device_id={axis: t}, device_id_type=pl.DeviceIdType.MESH
        )

    others(n, NARROW, signal("narrow"))
    others(w, WIDE, signal("wide"))
    return barrier


def greeted(barrier):
    pl.semaphore_wait(barrier, NARROW + WIDE - 2)


def loop(count, fn):
    def body(i, carry):
        fn(i)
        return carry

    lax.fori_loop(0, count, body, 0)


class Names:
    def __init__(self, names, refs):
        for name, ref in zip(names, refs):
            setattr(self, name, ref)


class Round:
    def __init__(self, axis, size, me, src, dst, send, recv):
        self.axis, self.size, self.me = axis, size, me
        self.src, self.dst, self.send, self.recv = src, dst, send, recv

    def start(self, whole=False):
        def one(t):
            remote(
                self.src if whole else self.src.at[t],
                self.dst.at[self.me],
                self.send,
                self.recv,
                {self.axis: t},
            ).start()

        others(self.me, self.size, one)

    def all_of(self):
        part = self.dst.at[pl.ds(0, self.size - 1)]
        return remote(part, part, self.send, self.recv, {self.axis: lax.rem(self.me + 1, self.size)})

    def arrived(self):
        self.all_of().wait_recv()

    def sent(self):
        self.all_of().wait_send()


FORWARD = dict(
    ys=pltpu.VMEM((CHUNKS, NARROW, ROWS, 1024), F32),
    yr=pltpu.VMEM((CHUNKS, NARROW, ROWS, 1024), F32),
    xs=pltpu.VMEM((WIDE, 8, 128), F32),
    xr=pltpu.VMEM((WIDE, 8, 128), F32),
    ms=pltpu.VMEM((WIDE, 1, 128), F32),
    mr=pltpu.VMEM((WIDE, 1, 128), F32),
    ysem=pltpu.SemaphoreType.DMA((2, CHUNKS)),
    xsem=pltpu.SemaphoreType.DMA((2,)),
    msem=pltpu.SemaphoreType.DMA((2,)),
)

INVERSE = dict(
    ns=pltpu.VMEM((WIDE, 1, 128), F32),
    nr=pltpu.VMEM((WIDE, 1, 128), F32),
    vs=pltpu.VMEM((WIDE, 8, 128), F32),
    vr=pltpu.VMEM((WIDE, 8, 128), F32),
    as_=pltpu.VMEM((CHUNKS, ROWS, 1024), F32),
    ar=pltpu.VMEM((CHUNKS, NARROW, ROWS, 1024), F32),
    nsem=pltpu.SemaphoreType.DMA((2,)),
    vsem=pltpu.SemaphoreType.DMA((2,)),
    asem=pltpu.SemaphoreType.DMA((2, CHUNKS)),
)


def depth_forward(field, zf):
    full = dot(field.reshape(YL * C, NZ), zf)
    full = (full[:, :128] + full[:, 128:]).reshape(YL, 4, 8, 128)
    lane = lane_of((YL, 8, 128))
    low = jnp.where(lane < 32, full[:, 0], full[:, 1])
    high = jnp.where(lane < 96, full[:, 2], full[:, 3])
    return jnp.where(lane < 64, low, high)


class Forward:
    def __init__(self, s, own, n, w):
        self.s, self.own, self.n, self.w = s, own, n, w
        self.x = Round("wide", WIDE, w, own.xs, own.xr, own.xsem.at[0], own.xsem.at[1])
        self.m = Round("wide", WIDE, w, own.ms, own.mr, own.msem.at[0], own.msem.at[1])

    def y(self, q):
        o = self.own
        return Round("narrow", NARROW, self.n, o.ys.at[q], o.yr.at[q], o.ysem.at[0, q], o.ysem.at[1, q])

    def put_rows(self, i, depth):
        s = self.s
        s.d[...] = depth.reshape(YL * 8, 128)
        rows = pl.multiple_of(i * 64, 64)
        turned = pl.multiple_of(i * 64 + 32, 32)
        for c8 in range(8):
            part = s.d[pl.ds(c8, YL, stride=8), :]
            lanes = slice(c8 * 128, c8 * 128 + 128)
            s.rh[pl.ds(rows, 32), lanes], s.rl[pl.ds(rows, 32), lanes] = halves(part)
            s.rh[pl.ds(turned, 32), lanes], s.rl[pl.ds(turned, 32), lanes] = halves(turn(part))

    def send_chunk(self, q):
        s, o = self.s, self.own
        out = dot3(s.yf, s.rh[...], s.rl[...])
        o.ys[q] = out.reshape(NARROW, ROWS, 1024)
        o.yr[q, self.n] = o.ys[q, self.n]
        self.y(q).start()

    def sum_chunks(self):
        o = self.own
        for q in range(CHUNKS):
            self.y(q).arrived()
            total = o.yr[q, 0]
            for t in range(1, NARROW):
                total = total + o.yr[q, t]
            for k in range(KY):
                for c8 in range(8):
                    o.xs[k * 8 + c8, q * XC : q * XC + XC] = total[
                        k * XC : k * XC + XC, c8 * 128 : c8 * 128 + 128
                    ]
        o.xr[self.w] = o.xs[self.w]
        self.x.start()

    def to_owner(self, xf):
        o = self.own
        self.x.arrived()
        cells = o.xr[...].reshape(256, 128)
        hi, lo = halves(jnp.concatenate((cells, turn(cells)), axis=0))
        o.ms[...] = dot3(xf, hi, lo).reshape(WIDE, 1, 128)
        o.mr[self.w] = o.ms[self.w]
        self.m.start()

    def modes(self):
        self.m.arrived()
        return self.own.mr[...].reshape(WIDE, 128)

    def finish(self):
        loop(CHUNKS, lambda q: self.y(q).sent())
        self.x.sent()
        self.m.sent()


class Inverse:
    def __init__(self, s, own, n, w):
        self.s, self.own, self.n, self.w = s, own, n, w
        self.m = Round("wide", WIDE, w, own.ns, own.nr, own.nsem.at[0], own.nsem.at[1])
        self.x = Round("wide", WIDE, w, own.vs, own.vr, own.vsem.at[0], own.vsem.at[1])

    def y(self, q):
        o = self.own
        return Round("narrow", NARROW, self.n, o.as_.at[q], o.ar.at[q], o.asem.at[0, q], o.asem.at[1, q])

    def start(self, modes):
        o = self.own
        o.ns[...] = modes.reshape(WIDE, 1, 128)
        o.nr[self.w] = o.ns[self.w]
        self.m.start()

    def to_cells(self, xi):
        o = self.own
        self.m.arrived()
        modes = o.nr[...].reshape(WIDE, 128)
        hi, lo = halves(jnp.concatenate((modes, turn(modes)), axis=0))
        o.vs[...] = dot3(xi, hi, lo).reshape(WIDE, 8, 128)
        o.vr[self.w] = o.vs[self.w]
        self.x.start()

    def gather(self):
        o = self.own
        self.x.arrived()
        for q in range(CHUNKS):
            for k in range(KY):
                for c8 in range(8):
                    o.as_[q, k * XC : k * XC + XC, c8 * 128 : c8 * 128 + 128] = o.vr[
                        k * 8 + c8, q * XC : q * XC + XC
                    ]
            o.ar[q, self.n] = o.as_[q]
            self.y(q).start(whole=True)

    def chunk(self, q):
        s, o = self.s, self.own
        self.y(q).arrived()
        columns = []
        for c8 in range(8):
            part = o.ar[q, :, :, c8 * 128 : c8 * 128 + 128].reshape(NARROW * ROWS, 128)
            columns.append(jnp.concatenate((part, turn(part)), axis=0))
        hi, lo = halves(jnp.concatenate(columns, axis=1))
        out = dot3(s.yi, hi, lo)
        for i in range(XC):
            for c8 in range(8):
                s.s[pl.ds(i * 256 + c8, YL, stride=8), :] = out[
                    i * YL : i * YL + YL, c8 * 128 : c8 * 128 + 128
                ]

    def field_row(self, i, zi):
        s = self.s
        hi, lo = halves(s.s[pl.ds(pl.multiple_of(i * 256, 256), 256), :])
        both = jnp.concatenate((hi, lo, hi), axis=1)
        for g in range(4):
            s.field[:, g] = dot(both, zi[g]).reshape(YL, 8, NZ)

    def finish(self):
        self.m.sent()
        self.x.sent()
        loop(CHUNKS, lambda q: self.y(q).sent())


def fold_point(full):
    row = lax.broadcasted_iota(jnp.int32, full.shape, 0) // 32
    full = jnp.where(row == lane_of(full.shape) // 32, full, 0.0)
    total = full[0:32]
    for y in range(1, 8):
        total = total + full[y * 32 : y * 32 + 32]
    total = total[:, :128] + total[:, 128:]
    total = total + pltpu.roll(total, 64, 1)
    total = total + pltpu.roll(total, 32, 1)
    lane = lane_of((8, 128))
    low = jnp.where(lane < 32, total[0:8], total[8:16])
    high = jnp.where(lane < 96, total[16:24], total[24:32])
    return jnp.where(lane < 64, low, high)


def gelu_slope(u):
    k = math.sqrt(2.0 / math.pi)
    square = u * u
    h = 0.5 * jnp.tanh(u * (k + (k * 0.044715) * square)) + 0.5
    return h + h * (1.0 - h) * (u * (2.0 * k + (6.0 * k * 0.044715) * square))


def spread(rows, j):
    return group_sum(jnp.where(lane_of(rows.shape) // 16 == j, rows, 0.0))


def group_sum(v):
    v = v + pltpu.roll(v, 64, 1)
    v = v + pltpu.roll(v, 32, 1)
    return v + pltpu.roll(v, 16, 1)


def mix_modes(s, modes, weight_ref):
    for j in range(8):
        s.rep[j] = spread(modes, j)

    def body(c8, carry):
        first, second = carry
        for g in range(4):
            weight = weight_ref[c8 * 4 + g].astype(F32)

            def rows(part):
                return jnp.concatenate(
                    [
                        jnp.broadcast_to(s.rep[2 * g + part, pl.ds(k * 8 + c8, 1), :], (8, 128))
                        for k in range(KY)
                    ],
                    axis=0,
                )

            first = first + rows(0) * weight
            second = second + rows(1) * weight
        return first, second

    zero = jnp.zeros((WIDE, 128), F32)
    first, second = lax.fori_loop(0, 8, body, (zero, zero))
    return first - turn(second)


def mix_back(s, grads, weight_ref):
    turned = turn(grads)

    def body(c8):
        for g in range(4):
            weight = weight_ref[c8 * 4 + g].astype(F32)
            for part, field in enumerate((grads, turned)):
                total = jnp.sum((field * weight).reshape(KY, 8, 128), axis=1)
                for k in range(KY):
                    s.back[2 * g + part, k, pl.ds(c8, 1), :] = total[k : k + 1]

    loop(8, body)
    out = jnp.zeros((WIDE, 128), F32)
    for j in range(8):
        whole = group_sum(s.back[j].reshape(WIDE, 128))
        out = jnp.where(lane_of(out.shape) // 16 == j, whole, out)
    return out


def kernel(
    names,
    act_hbm,
    cot_hbm,
    point_ref,
    bias_ref,
    weight_ref,
    yf_hbm,
    yi_hbm,
    xf_ref,
    xi_ref,
    zf_ref,
    ziw_ref,
    zi1_ref,
    out_hbm,
    total_ref,
    coeffs_ref,
    grads_ref,
    *refs,
):
    s = Names(names, refs)
    n, w = lax.axis_index("narrow"), lax.axis_index("wide")

    def group(prefix, keys):
        keys = tuple(keys)
        return Names(keys, [getattr(s, prefix + key) for key in keys])

    ahead = Forward(s, group("f1_", FORWARD), n, w)
    grad = Forward(s, group("f2_", FORWARD), n, w)
    mixed_in = Inverse(s, group("i1_", INVERSE), n, w)
    back_in = Inverse(s, group("i2_", INVERSE), n, w)

    def act_copy(x):
        return pltpu.make_async_copy(act_hbm.at[x], s.act.at[x], s.act_sem.at[x])

    def cot_copy(x):
        return pltpu.make_async_copy(cot_hbm.at[x], s.cot.at[x], s.cot_sem.at[x])

    def out_copy(x):
        return pltpu.make_async_copy(s.out.at[x], out_hbm.at[x], s.out_sem.at[x])

    table_in = [
        pltpu.make_async_copy(yf_hbm.at[n], s.yf, s.table_sem.at[0]),
        pltpu.make_async_copy(yi_hbm.at[n], s.yi, s.table_sem.at[1]),
    ]
    barrier = greet(n, w)
    loop(XL, lambda x: act_copy(x).start())
    for copy in table_in:
        copy.start()
    loop(XL, lambda x: cot_copy(x).start())
    for copy in table_in:
        copy.wait()

    def forward_chunk(q):
        def row(i):
            x = q * XC + i
            act_copy(x).wait()
            ahead.put_rows(i, depth_forward(s.act[x], zf_ref[...]))

        loop(XC, row)

        @pl.when(q == 0)
        def _():
            greeted(barrier)

        ahead.send_chunk(q)

    loop(CHUNKS, forward_chunk)

    row = lax.broadcasted_iota(jnp.int32, (256, 32), 0)
    pick = lax.rem(row, 32) == lane_of((256, 32))
    ones = jnp.where(pick, 1.0, 0.0).astype(BF16)
    bias_rows = jnp.sum(jnp.where(pick, bias_ref[...], 0.0), axis=1, keepdims=True)
    same = lax.broadcasted_iota(jnp.int32, (256, 256), 0) // 32 == lane_of((256, 256)) // 32
    tall = dot(ones, point_ref[...]).astype(BF16)
    s.mix_back[...] = jnp.where(same, dot_t(tall, ones), 0.0).astype(BF16)
    tall = dot_t(ones, point_ref[...]).astype(BF16)
    s.mix[...] = jnp.where(same, dot_t(tall, ones), 0.0).astype(BF16)

    def blocks(fn):
        def one(i):
            fn(i // 4, pl.ds(pl.multiple_of(lax.rem(i, 4) * 8, 8), 8))

        loop(4 * XL, one)

    def mix_block(x, ys):
        point = dot(s.mix[...], s.act[x, ys].reshape(256, NZ)) + bias_rows
        s.point[x, ys] = point.reshape(8, C, NZ)

    blocks(mix_block)
    ahead.sum_chunks()
    ahead.to_owner(xf_ref)
    coeffs = ahead.modes()
    mixed_in.start(mix_modes(s, coeffs, weight_ref))
    coeffs_ref[...] = ahead.own.mr[...]
    s.bs[...] = jnp.zeros_like(s.bs)
    s.pg[...] = jnp.zeros_like(s.pg)
    mixed_in.to_cells(xi_ref)
    mixed_in.gather()

    def middle_chunk(q):
        mixed_in.chunk(q)

        def row(i):
            x = q * XC + i
            cot_copy(x).wait()
            mixed_in.field_row(i, ziw_ref)

            def block(b):
                ys = pl.ds(pl.multiple_of(b * 8, 8), 8)
                preact = s.field[ys].reshape(256, NZ) + s.point[x, ys].reshape(256, NZ)
                cot = s.cot[x, ys].reshape(256, NZ).astype(F32)
                pre = (cot * gelu_slope(preact)).astype(BF16)
                s.pre[x, ys] = pre.reshape(8, C, NZ)

            loop(4, block)
            depth = depth_forward(s.pre[x], zf_ref[...])
            s.bs[...] += jnp.sum(depth, axis=0)
            grad.put_rows(i, depth)

        loop(XC, row)
        grad.send_chunk(q)

    loop(CHUNKS, middle_chunk)

    def back_block(x, ys):
        pre = s.pre[x, ys].reshape(256, NZ)
        s.pg[...] += dot_t(s.act[x, ys].reshape(256, NZ), pre)
        s.point[x, ys] = dot(s.mix_back[...], pre).reshape(8, C, NZ)

    blocks(back_block)
    s.ps[0:8] = fold_point(s.pg[...])
    s.ps[8:16] = s.bs[...]
    s.pr[n] = s.ps[...]
    grad.sum_chunks()
    narrow_sum = Round("narrow", NARROW, n, s.ps, s.pr, s.psem.at[0], s.psem.at[1])
    narrow_sum.start(whole=True)
    grad.to_owner(xf_ref)
    narrow_sum.arrived()
    total = s.pr[0]
    for t in range(1, NARROW):
        total = total + s.pr[t]
    s.ts[...] = total
    s.tr[w] = total
    rows = grad.modes()
    depth_weight = jnp.where(lax.rem(lane_of(rows.shape), 16) == 0, 1.0, 2.0)
    grads = rows * depth_weight
    back_in.start(mix_back(s, grads, weight_ref))
    grads_ref[...] = grads.reshape(WIDE, 1, 128)
    back_in.to_cells(xi_ref)
    wide_sum = Round("wide", WIDE, w, s.ts, s.tr, s.tsem.at[0], s.tsem.at[1])
    back_in.gather()
    wide_sum.start(whole=True)

    def last_chunk(q):
        back_in.chunk(q)

        def row(i):
            x = q * XC + i
            back_in.field_row(i, zi1_ref)

            def block(b):
                ys = pl.ds(pl.multiple_of(b * 8, 8), 8)
                out = s.field[ys].reshape(256, NZ) + s.point[x, ys].reshape(256, NZ)
                s.out[x, ys] = out.astype(BF16).reshape(8, C, NZ)

            loop(4, block)
            out_copy(x).start()

        loop(XC, row)

    loop(CHUNKS, last_chunk)
    wide_sum.arrived()
    total = s.tr[0]
    for t in range(1, WIDE):
        total = total + s.tr[t]
    total_ref[...] = total
    for part in (ahead, grad, mixed_in, back_in):
        part.finish()
    narrow_sum.sent()
    wide_sum.sent()
    loop(XL, lambda x: out_copy(x).wait())


VM = pl.BlockSpec(memory_space=pltpu.VMEM)
HB = pl.BlockSpec(memory_space=pl.ANY)
FIELD = (XL, YL, C, NZ)


def local(activations, cotangent, point_weight, bias, spectral_weight):
    tabs = {name: jnp.asarray(value) for name, value in tables().items()}
    weight = (
        spectral_weight.reshape(2, KY, M, 4, 8, 4, 8)
        .transpose(4, 3, 1, 6, 5, 0, 2)
        .reshape(C, WIDE, 128)
    )
    scratch = dict(
        act=pltpu.VMEM(FIELD, BF16),
        cot=pltpu.VMEM(FIELD, BF16),
        pre=pltpu.VMEM(FIELD, BF16),
        out=pltpu.VMEM(FIELD, BF16),
        point=pltpu.VMEM(FIELD, F32),
        field=pltpu.VMEM((YL, 4, 8, NZ), F32),
        d=pltpu.VMEM((256, 128), F32),
        rh=pltpu.VMEM((64 * XC, 1024), BF16),
        rl=pltpu.VMEM((64 * XC, 1024), BF16),
        s=pltpu.VMEM((XC * 256, 128), F32),
        yf=pltpu.VMEM((2, 32 * XC, 64 * XC), BF16),
        yi=pltpu.VMEM((2, 32 * XC, 64 * XC), BF16),
        mix=pltpu.VMEM((256, 256), BF16),
        mix_back=pltpu.VMEM((256, 256), BF16),
        rep=pltpu.VMEM((8, WIDE, 128), F32),
        back=pltpu.VMEM((8, KY, 8, 128), F32),
        pg=pltpu.VMEM((256, 256), F32),
        bs=pltpu.VMEM((8, 128), F32),
        ps=pltpu.VMEM((16, 128), F32),
        pr=pltpu.VMEM((NARROW, 16, 128), F32),
        ts=pltpu.VMEM((16, 128), F32),
        tr=pltpu.VMEM((WIDE, 16, 128), F32),
        act_sem=pltpu.SemaphoreType.DMA((XL,)),
        cot_sem=pltpu.SemaphoreType.DMA((XL,)),
        out_sem=pltpu.SemaphoreType.DMA((XL,)),
        table_sem=pltpu.SemaphoreType.DMA((2,)),
        psem=pltpu.SemaphoreType.DMA((2,)),
        tsem=pltpu.SemaphoreType.DMA((2,)),
    )
    for prefix, group in (("f1_", FORWARD), ("f2_", FORWARD), ("i1_", INVERSE), ("i2_", INVERSE)):
        scratch.update({prefix + key: value for key, value in group.items()})
    input_grad, total, coeffs, grads = pl.pallas_call(
        functools.partial(kernel, tuple(scratch)),
        name="layer_backward",
        in_specs=[HB, HB, VM, VM, VM, HB, HB, VM, VM, VM, VM, VM],
        out_specs=[HB, VM, VM, VM],
        out_shape=[
            jax.ShapeDtypeStruct(FIELD, BF16),
            jax.ShapeDtypeStruct((16, 128), F32),
            jax.ShapeDtypeStruct((WIDE, 1, 128), F32),
            jax.ShapeDtypeStruct((WIDE, 1, 128), F32),
        ],
        scratch_shapes=tuple(scratch.values()),
        compiler_params=pltpu.CompilerParams(
            collective_id=0, has_side_effects=True, vmem_limit_bytes=56 * 1024 * 1024
        ),
    )(
        activations,
        cotangent,
        point_weight,
        bias[None],
        weight,
        *(tabs[name] for name in ("yf", "yi", "xf", "xi", "zf", "ziw", "zi1")),
    )

    def modes_in(rows):
        return rows.reshape(KY, 8, 4, 2, M).transpose(3, 0, 4, 2, 1).reshape(2, KY, M, C)

    coeffs, grads = modes_in(coeffs), modes_in(grads)
    cr, ci = coeffs[0][..., :, None], coeffs[1][..., :, None]
    gr, gi = grads[0][..., None, :], grads[1][..., None, :]
    spectral_grad = jnp.stack((cr * gr + ci * gi, cr * gi - ci * gr))[:, None]
    point_grad = total[0:8].reshape(8, 4, C).transpose(1, 0, 2).reshape(C, C) * SCALE
    bias_grad = total[8:16].reshape(8, 4, 2, M)[:, :, 0, 0].T.reshape(C) * SCALE
    return (input_grad, point_grad, bias_grad, spectral_grad)


def solution(mesh):
    return jax.shard_map(
        local,
        mesh=mesh,
        in_specs=(
            P("wide", "narrow", None, None),
            P("wide", "narrow", None, None),
            P(),
            P(),
            P(None, "wide", "narrow", None, None, None),
        ),
        out_specs=(
            P("wide", "narrow", None, None),
            P(),
            P(),
            P(None, "wide", "narrow", None, None, None),
        ),
        check_vma=False,
    )
```

time: 2130 us -> 149 us (0.07)
  waiting for transfers between devices: 1850 us -> 0 us
  Pallas kernels: 0 us -> 126 us
  matrix products: 120 us -> 0 us
  blocking collectives: 78.3 us -> 0 us
  local copies, waits for them, and re-layouts: 44.2 us -> 16.2 us
    all_gather x2 -> x0, waiting for transfers between devices: 1320 us -> none  [to_field(): lax.all_gather(modes.reshape(local_x * local_y, 2, features), ('wide', 'n...]
    unnamed x6 -> x0, waiting for transfers between devices: 537 us -> none
    pallas_call x0 -> x1, Pallas kernels: none -> 126 us  [local(): pl.pallas_call(functools.partial(kernel, tuple(scratch)), name='layer_bac...]
    dot_general x43 -> x0, matrix products: 120 us -> none  [the longest x40 102 us: contract(): jnp.einsum(form, left, right, precision=lax.Precision.HIGH, preferred_ele...]
    psum x1 -> x0, blocking collectives: 78.3 us -> none  [local(): lax.psum((weight_sum, bias_sum), ('wide', 'narrow'))]
  transfers between devices with their start and end apart: 4 -> 0, of which waited for: 4 -> 0; matrix products, arithmetic and copies ran while one was open for 1% -> 0% of each run, Pallas kernels for 0% -> 0%
where the time goes in v2:
time: 149 us; the launch traced here: 148 us
  Pallas kernels  126 us (85%)
  local copies, waits for them, and re-layouts  16.2 us (11%)
  other arithmetic  5.71 us (4%)
    pallas_call x1, Pallas kernels, local(): pl.pallas_call(functools.partial(kernel, tuple(scratch)), name='layer_bac...  126 us
    unnamed x5, local copies, waits for them, and re-layouts  6.63 us
    transpose x1, local copies, waits for them, and re-layouts, local(): weight = spectral_weight.reshape(2, KY, M, 4, 8, 4, 8).transpose(4, 3, 1,...  4.83 us

profile of v2, /device:TPU:1, one launch (start us, length us, event | category | flops | bytes accessed | tf_op | source)
XLA Modules:
  0.0 148.4 jit_solution(16811921964215512173)
XLA Ops:
  0.6 3.2 %copy.19 = bf16[2,1,4,16,32,32]{3,5,4,2,0,1:T(8,128)(2,1)} copy(bf16[2,1,4,16,32,32]{5,4,3,2,1,0:T(8,128)(2,1)} %param.16) | data formatting | bytes 524288 | tf_op args[4]
  3.8 4.8 %copy.20 = bf16[8,4,4,8,4,2,16]{6,5,4,3,2,1,0:T(2,128)(2,1)S(1)} copy(bf16[8,4,4,8,4,2,16]{6,3,4,0,1,2,5:T(8,128)(2,1)} %bitcast.28) | data formatting | bytes 524288 | tf_op jit(solution)/shard_map/transpose | solution.py:618
  8.6 2.1 %reshape.67.weight_ref = bf16[32,32,128]{2,1,0:T(8,128)(2,1)} reshape(bf16[8,4,4,8,4,2,16]{6,5,4,3,2,1,0:T(2,128)(2,1)S(1)} %copy.20) | data formatting | bytes 524288 | tf_op jit(solution)/shard_map/reshape | solution.py:619
  10.7 125.8 %layer_backward.1 = (bf16[8,32,32,256]{3,2,1,0:T(8,128)(2,1)}, f32[16,128]{1,0:T(8,128)}, f32[32,1,128]{2,1,0:T(1,128)}, f32[32,1,128]{2,1,0:T(1,128)}) custom-call(bf16[8,32,32,256]{3,2,1,0:T(8,128)(2,1)} %act_hbm.1, bf16[8,32,32,256]{3,2,1,0:T(8,128)(2,1)} %cot_hbm.1, bf16[32,32]{1,0:T(8,128)(2,1)} %point_ref.1, f32[1,32]{1,0:T(1,128)} %bitcast.33, ...), custom_call_target="tpu_custom_call" | custom-call | tf_op jit(solution)/shard_map/layer_backward/pallas_call | solution.py:653
  136.4 0.7 fusion
  137.1 0.1 mul.112
  137.2 0.6 copy.35
  137.8 0.1 reshape.68
  138.0 0.1 copy.29
  138.1 0.6 mul.119
  138.7 0.5 broadcast.74
  139.2 1.4 reduce.6
  140.6 0.2 reshape.70
  140.9 0.1 copy.28
  140.9 1.4 reduce.7
  142.3 0.2 reshape.69
  142.6 0.1 copy.27
  142.7 0.1 copy.26
  142.8 0.1 copy.24
  142.8 0.6 multiply_add_fusion
  143.5 0.0 copy-start
  143.5 1.6 %maximum_bitcast_fusion = f32[2,1,4,16,32,32]{5,4,3,2,1,0:T(8,128)} fusion(f32[1,4,16,32,32]{4,3,2,1,0:T(8,128)S(1)} %get-tuple-element.13, f32[1,4,16,32,32]{4,3,2,1,0:T(8,128)S(1)} %get-tuple-element.12), kind=kLoop, calls=%fused_computation | loop fusion | flops 131072 | bytes 1048576 | tf_op jit(solution)/shard_map/broadcast_in_dim | solution.py:683
  145.1 1.4 copy-done
  146.4 2.0 %copy.37 = bf16[8,32,32,256]{3,2,1,0:T(8,128)(2,1)} copy(bf16[8,32,32,256]{3,2,1,0:T(8,128)(2,1)S(1)} %copy-done) | data formatting | bytes 8388608
  (6 shorter events, 0.1 us)
Async XLA Ops:
  143.5 2.9 %copy-start = (bf16[8,32,32,256]{3,2,1,0:T(8,128)(2,1)S(1)}, bf16[8,32,32,256]{3,2,1,0:T(8,128)(2,1)}, u32[]{:S(2)}) copy-start(bf16[8,32,32,256]{3,2,1,0:T(8,128)(2,1)} %get-tuple-element.24) | copy-start | bytes 12582916

commit v3 on v2

--- a/solution.py
+++ b/solution.py
@@ -366,60 +366,78 @@
     return h + h * (1.0 - h) * (u * (2.0 * k + (6.0 * k * 0.044715) * square))
 
 
-def spread(rows, j):
-    return group_sum(jnp.where(lane_of(rows.shape) // 16 == j, rows, 0.0))
-
-
-def group_sum(v):
-    v = v + pltpu.roll(v, 64, 1)
-    v = v + pltpu.roll(v, 32, 1)
-    return v + pltpu.roll(v, 16, 1)
-
-
-def mix_modes(s, modes, weight_ref):
-    for j in range(8):
-        s.rep[j] = spread(modes, j)
-
-    def body(c8, carry):
-        first, second = carry
-        for g in range(4):
-            weight = weight_ref[c8 * 4 + g].astype(F32)
-
-            def rows(part):
-                return jnp.concatenate(
-                    [
-                        jnp.broadcast_to(s.rep[2 * g + part, pl.ds(k * 8 + c8, 1), :], (8, 128))
-                        for k in range(KY)
-                    ],
-                    axis=0,
-                )
-
-            first = first + rows(0) * weight
-            second = second + rows(1) * weight
-        return first, second
-
-    zero = jnp.zeros((WIDE, 128), F32)
-    first, second = lax.fori_loop(0, 8, body, (zero, zero))
-    return first - turn(second)
-
-
-def mix_back(s, grads, weight_ref):
-    turned = turn(grads)
-
-    def body(c8):
-        for g in range(4):
-            weight = weight_ref[c8 * 4 + g].astype(F32)
-            for part, field in enumerate((grads, turned)):
-                total = jnp.sum((field * weight).reshape(KY, 8, 128), axis=1)
-                for k in range(KY):
-                    s.back[2 * g + part, k, pl.ds(c8, 1), :] = total[k : k + 1]
-
-    loop(8, body)
-    out = jnp.zeros((WIDE, 128), F32)
-    for j in range(8):
-        whole = group_sum(s.back[j].reshape(WIDE, 128))
-        out = jnp.where(lane_of(out.shape) // 16 == j, whole, out)
-    return out
+def by_channel(rows):
+    return jnp.concatenate(
+        [
+            pltpu.roll(rows[k * 8 : k * 8 + 8], (128 - 32 * g) % 128, 1)
+            for k in range(KY)
+            for g in range(4)
+        ],
+        axis=0,
+    )
+
+
+def by_group(pieces):
+    lane = lane_of((8, 128))
+    rows = []
+    for k in range(KY):
+        low = jnp.where(lane < 32, pieces(k, 0), pieces(k, 1))
+        high = jnp.where(lane < 96, pieces(k, 2), pieces(k, 3))
+        rows.append(jnp.where(lane < 64, low, high))
+    return jnp.concatenate(rows, axis=0)
+
+
+def mix_modes(s, modes):
+    def body(kz, columns):
+        for k in range(KY):
+            rows = columns[k * C : k * C + C]
+            real, imag = rows[:, 0:1], rows[:, M : M + 1]
+            w_real, w_imag = s.weight[0, k, kz].astype(F32), s.weight[1, k, kz].astype(F32)
+            s.mt[k, pl.ds(kz, 1), :C] = jnp.sum(real * w_real - imag * w_imag, axis=0, keepdims=True)
+            s.mt[k, pl.ds(kz + M, 1), :C] = jnp.sum(
+                real * w_imag + imag * w_real, axis=0, keepdims=True
+            )
+        return pltpu.roll(columns, 127, 1)
+
+    s.mt[...] = jnp.zeros_like(s.mt)
+    lax.fori_loop(0, M, body, by_channel(modes))
+    turned = s.mt[...].reshape(KY * 2 * M, 128).T
+    return by_group(
+        lambda k, g: pltpu.roll(turned[g * 8 : g * 8 + 8], (128 + 32 * (g - k)) % 128, 1)
+    )
+
+
+def mix_back(s, grads):
+    turned = by_channel(grads).T
+    for k in range(KY):
+        s.gt[k] = pltpu.roll(turned[: 2 * M], (128 - 32 * k) % 128, 1)
+    lane = lane_of((C, 128))
+
+    def body(kz, totals):
+        out = []
+        for k in range(KY):
+            real, imag = s.gt[k, pl.ds(kz, 1), :C], s.gt[k, pl.ds(kz + M, 1), :C]
+            w_real, w_imag = s.weight[0, k, kz].astype(F32), s.weight[1, k, kz].astype(F32)
+            first = jnp.sum(real * w_real + imag * w_imag, axis=1, keepdims=True)
+            second = jnp.sum(imag * w_real - real * w_imag, axis=1, keepdims=True)
+            out.append(jnp.where(lane == kz, first, jnp.where(lane == kz + M, second, totals[k])))
+        return tuple(out)
+
+    totals = lax.fori_loop(0, M, body, tuple(jnp.zeros((C, 128), F32) for _ in range(KY)))
+    return by_group(lambda k, g: pltpu.roll(totals[k][g * 8 : g * 8 + 8], 32 * g, 1))
+
+
+def outer_modes(s, modes):
+    def body(kz, columns):
+        for k in range(KY):
+            rows = columns[k * C : k * C + C]
+            real, imag = rows[:, 0:1], rows[:, M : M + 1]
+            g_real, g_imag = s.gt[k, pl.ds(kz, 1), :C], s.gt[k, pl.ds(kz + M, 1), :C]
+            s.sg[0, k, kz] = real * g_real + imag * g_imag
+            s.sg[1, k, kz] = real * g_imag - imag * g_real
+        return pltpu.roll(columns, 127, 1)
+
+    lax.fori_loop(0, M, body, by_channel(modes))
 
 
 def kernel(
@@ -428,7 +446,7 @@
     cot_hbm,
     point_ref,
     bias_ref,
-    weight_ref,
+    weight_hbm,
     yf_hbm,
     yi_hbm,
     xf_ref,
@@ -437,9 +455,9 @@
     ziw_ref,
     zi1_ref,
     out_hbm,
-    total_ref,
-    coeffs_ref,
-    grads_ref,
+    point_grad_ref,
+    bias_grad_ref,
+    sg_hbm,
     *refs,
 ):
     s = Names(names, refs)
@@ -467,10 +485,13 @@
         pltpu.make_async_copy(yf_hbm.at[n], s.yf, s.table_sem.at[0]),
         pltpu.make_async_copy(yi_hbm.at[n], s.yi, s.table_sem.at[1]),
     ]
+    weight_copy = pltpu.make_async_copy(weight_hbm.at[:, 0], s.weight, s.table_sem.at[2])
+    sg_copy = pltpu.make_async_copy(s.sg, sg_hbm.at[:, 0], s.table_sem.at[3])
     barrier = greet(n, w)
     loop(XL, lambda x: act_copy(x).start())
     for copy in table_in:
         copy.start()
+    weight_copy.start()
     loop(XL, lambda x: cot_copy(x).start())
     for copy in table_in:
         copy.wait()
@@ -514,9 +535,8 @@
     blocks(mix_block)
     ahead.sum_chunks()
     ahead.to_owner(xf_ref)
-    coeffs = ahead.modes()
-    mixed_in.start(mix_modes(s, coeffs, weight_ref))
-    coeffs_ref[...] = ahead.own.mr[...]
+    weight_copy.wait()
+    mixed_in.start(mix_modes(s, ahead.modes()))
     s.bs[...] = jnp.zeros_like(s.bs)
     s.pg[...] = jnp.zeros_like(s.pg)
     mixed_in.to_cells(xi_ref)
@@ -569,8 +589,9 @@
     rows = grad.modes()
     depth_weight = jnp.where(lax.rem(lane_of(rows.shape), 16) == 0, 1.0, 2.0)
     grads = rows * depth_weight
-    back_in.start(mix_back(s, grads, weight_ref))
-    grads_ref[...] = grads.reshape(WIDE, 1, 128)
+    back_in.start(mix_back(s, grads))
+    outer_modes(s, ahead.own.mr[...].reshape(WIDE, 128))
+    sg_copy.start()
     back_in.to_cells(xi_ref)
     wide_sum = Round("wide", WIDE, w, s.ts, s.tr, s.tsem.at[0], s.tsem.at[1])
     back_in.gather()
@@ -598,11 +619,18 @@
     total = s.tr[0]
     for t in range(1, WIDE):
         total = total + s.tr[t]
-    total_ref[...] = total
+    for g in range(4):
+        point_grad_ref[g * 8 : g * 8 + 8] = SCALE * total[0:8, g * 32 : g * 32 + C]
+    row, lane = lax.broadcasted_iota(jnp.int32, (8, C), 0), lane_of((8, C))
+    bias_grad = jnp.zeros((8, C), F32)
+    for g in range(4):
+        bias_grad = jnp.where(lane == g * 8 + row, total[8:16, g * 32 : g * 32 + 1], bias_grad)
+    bias_grad_ref[...] = SCALE * jnp.sum(bias_grad, axis=0, keepdims=True)
     for part in (ahead, grad, mixed_in, back_in):
         part.finish()
     narrow_sum.sent()
     wide_sum.sent()
+    sg_copy.wait()
     loop(XL, lambda x: out_copy(x).wait())
 
 
@@ -613,11 +641,6 @@
 
 def local(activations, cotangent, point_weight, bias, spectral_weight):
     tabs = {name: jnp.asarray(value) for name, value in tables().items()}
-    weight = (
-        spectral_weight.reshape(2, KY, M, 4, 8, 4, 8)
-        .transpose(4, 3, 1, 6, 5, 0, 2)
-        .reshape(C, WIDE, 128)
-    )
     scratch = dict(
         act=pltpu.VMEM(FIELD, BF16),
         cot=pltpu.VMEM(FIELD, BF16),
@@ -633,8 +656,10 @@
         yi=pltpu.VMEM((2, 32 * XC, 64 * XC), BF16),
         mix=pltpu.VMEM((256, 256), BF16),
         mix_back=pltpu.VMEM((256, 256), BF16),
-        rep=pltpu.VMEM((8, WIDE, 128), F32),
-        back=pltpu.VMEM((8, KY, 8, 128), F32),
+        weight=pltpu.VMEM((2, KY, M, C, C), BF16),
+        sg=pltpu.VMEM((2, KY, M, C, C), F32),
+        mt=pltpu.VMEM((KY, 2 * M, 128), F32),
+        gt=pltpu.VMEM((KY, 2 * M, 128), F32),
         pg=pltpu.VMEM((256, 256), F32),
         bs=pltpu.VMEM((8, 128), F32),
         ps=pltpu.VMEM((16, 128), F32),
@@ -644,22 +669,22 @@
         act_sem=pltpu.SemaphoreType.DMA((XL,)),
         cot_sem=pltpu.SemaphoreType.DMA((XL,)),
         out_sem=pltpu.SemaphoreType.DMA((XL,)),
-        table_sem=pltpu.SemaphoreType.DMA((2,)),
+        table_sem=pltpu.SemaphoreType.DMA((4,)),
         psem=pltpu.SemaphoreType.DMA((2,)),
         tsem=pltpu.SemaphoreType.DMA((2,)),
     )
     for prefix, group in (("f1_", FORWARD), ("f2_", FORWARD), ("i1_", INVERSE), ("i2_", INVERSE)):
         scratch.update({prefix + key: value for key, value in group.items()})
-    input_grad, total, coeffs, grads = pl.pallas_call(
+    input_grad, point_grad, bias_grad, spectral_grad = pl.pallas_call(
         functools.partial(kernel, tuple(scratch)),
         name="layer_backward",
-        in_specs=[HB, HB, VM, VM, VM, HB, HB, VM, VM, VM, VM, VM],
-        out_specs=[HB, VM, VM, VM],
+        in_specs=[HB, HB, VM, VM, HB, HB, HB, VM, VM, VM, VM, VM],
+        out_specs=[HB, VM, VM, HB],
         out_shape=[
             jax.ShapeDtypeStruct(FIELD, BF16),
-            jax.ShapeDtypeStruct((16, 128), F32),
-            jax.ShapeDtypeStruct((WIDE, 1, 128), F32),
-            jax.ShapeDtypeStruct((WIDE, 1, 128), F32),
+            jax.ShapeDtypeStruct((C, C), F32),
+            jax.ShapeDtypeStruct((1, C), F32),
+            jax.ShapeDtypeStruct((2, 1, KY, M, C, C), F32),
         ],
         scratch_shapes=tuple(scratch.values()),
         compiler_params=pltpu.CompilerParams(
@@ -670,20 +695,11 @@
         cotangent,
         point_weight,
         bias[None],
-        weight,
+        spectral_weight,
         *(tabs[name] for name in ("yf", "yi", "xf", "xi", "zf", "ziw", "zi1")),
     )
 
-    def modes_in(rows):
-        return rows.reshape(KY, 8, 4, 2, M).transpose(3, 0, 4, 2, 1).reshape(2, KY, M, C)
-
-    coeffs, grads = modes_in(coeffs), modes_in(grads)
-    cr, ci = coeffs[0][..., :, None], coeffs[1][..., :, None]
-    gr, gi = grads[0][..., None, :], grads[1][..., None, :]
-    spectral_grad = jnp.stack((cr * gr + ci * gi, cr * gi - ci * gr))[:, None]
-    point_grad = total[0:8].reshape(8, 4, C).transpose(1, 0, 2).reshape(C, C) * SCALE
-    bias_grad = total[8:16].reshape(8, 4, 2, M)[:, :, 0, 0].T.reshape(C) * SCALE
-    return (input_grad, point_grad, bias_grad, spectral_grad)
+    return (input_grad, point_grad, bias_grad.reshape(C), spectral_grad)
 
 
 def solution(mesh):

time: 149 us -> 137 us (0.919)
  local copies, waits for them, and re-layouts: 16.2 us -> 7.24 us
  other arithmetic: 5.71 us -> 0 us
  Pallas kernels: 126 us -> 129 us
    transpose x1 -> x0, local copies, waits for them, and re-layouts: 4.83 us -> none  [local(): weight = spectral_weight.reshape(2, KY, M, 4, 8, 4, 8).transpose(4, 3, 1,...]
    pallas_call x1, Pallas kernels: 126 us -> 129 us  [local(): pl.pallas_call(functools.partial(kernel, tuple(scratch)), name='layer_bac...]
    pallas_call x2 -> x0, other arithmetic: 2.81 us -> none  [local(): pl.pallas_call(functools.partial(kernel, tuple(scratch)), name='layer_bac...]
    reshape x6 -> x0, local copies, waits for them, and re-layouts: 2.64 us -> none  [the longest x1 2.06 us: local(): weight = spectral_weight.reshape(2, KY, M, 4, 8, 4, 8).transpose(4, 3, 1,...]
    mul x9 -> x0, local copies, waits for them, and re-layouts: 1.62 us -> none  [the longest x2 0.69 us: local(): total[0:8].reshape(8, 4, C).transpose(1, 0, 2).reshape(C, C) * SCALE]
    broadcast_in_dim x1 -> x0, other arithmetic: 1.58 us -> none  [local(): spectral_grad = jnp.stack((cr * gr + ci * gi, cr * gi - ci * gr))[:, None]]
    unnamed x5 -> x10, local copies, waits for them, and re-layouts: 6.63 us -> 7.24 us
where the time goes in v3:
time: 137 us
  Pallas kernels  129 us (94%)
  local copies, waits for them, and re-layouts  7.24 us (5%)
    pallas_call x1, Pallas kernels, local(): pl.pallas_call(functools.partial(kernel, tuple(scratch)), name='layer_bac...  129 us
    unnamed x10, local copies, waits for them, and re-layouts  7.24 us

profile of v3, /device:TPU:1, one launch (start us, length us, event | category | flops | bytes accessed | tf_op | source)
XLA Modules:
  0.0 137.4 jit_solution(8149055078920498246)
XLA Ops:
  0.6 129.5 %layer_backward.1 = (bf16[8,32,32,256]{3,2,1,0:T(8,128)(2,1)}, f32[32,32]{1,0:T(8,128)}, f32[1,32]{1,0:T(1,128)}, f32[2,1,4,16,32,32]{5,4,3,2,1,0:T(8,128)}) custom-call(bf16[8,32,32,256]{3,2,1,0:T(8,128)(2,1)} %act_hbm.1, bf16[8,32,32,256]{3,2,1,0:T(8,128)(2,1)} %cot_hbm.1, bf16[32,32]{1,0:T(8,128)(2,1)} %point_ref.1, f32[1,32]{1,0:T(1,128)} %bitcast.2, ...), custom_call_target="tpu_custom_call" | custom-call | tf_op jit(solution)/shard_map/layer_backward/pallas_call | solution.py:678
  130.1 0.0 copy-start.1
  130.1 0.0 copy-start.2
  130.1 0.0 copy-start
  130.1 4.8 %copy.20 = bf16[8,32,32,256]{3,2,1,0:T(8,128)(2,1)} copy(bf16[8,32,32,256]{3,2,1,0:T(8,128)(2,1)} %get-tuple-element.16) | data formatting | bytes 8388608
  134.9 0.0 copy-done.1
  134.9 0.6 copy.21
  135.5 0.0 copy-done.2
  135.5 0.5 copy.22
  136.1 0.0 copy-done
  136.1 1.3 copy.23
Async XLA Ops:
  130.1 4.8 %copy-start.1 = (f32[32,32]{1,0:T(8,128)S(1)}, f32[32,32]{1,0:T(8,128)}, u32[]{:S(2)}) copy-start(f32[32,32]{1,0:T(8,128)} %get-tuple-element.17) | copy-start | bytes 12292
  130.1 5.4 %copy-start.2 = (f32[1,32]{1,0:T(1,128)S(1)}, f32[1,32]{1,0:T(1,128)}, u32[]{:S(2)}) copy-start(f32[1,32]{1,0:T(1,128)} %get-tuple-element.10) | copy-start | bytes 388
  130.1 5.9 %copy-start = (f32[2,1,4,16,32,32]{5,4,3,2,1,0:T(8,128)S(1)}, f32[2,1,4,16,32,32]{5,4,3,2,1,0:T(8,128)}, u32[]{:S(2)}) copy-start(f32[2,1,4,16,32,32]{5,4,3,2,1,0:T(8,128)} %get-tuple-element.19) | copy-start | bytes 1572868

commit v4 on v3

--- a/solution.py
+++ b/solution.py
@@ -56,17 +56,25 @@
     yi = np.einsum("dtkny,xu->nxydtku", both, eye_x).reshape(NARROW, 32 * XC, 64 * XC)
     xf = np.concatenate((cos_a, sin_a), axis=1) * SCALE
     xi = np.concatenate((cos_a.T, -sin_a.T), axis=1)
-    zf = np.tile(np.concatenate((cos_z, -sin_z), axis=0).T, (1, 4))
+    parts = np.stack((cos_z, -sin_z)).reshape(2, 8, 2, NZ)
+    zf = np.broadcast_to(parts.transpose(3, 1, 0, 2)[:, :, None], (NZ, 8, 4, 2, 2)).reshape(NZ, 128)
     depth = np.where(np.arange(M) == 0, 1.0, 2.0)[:, None]
 
     def inverse_z(weights):
-        one = np.concatenate((cos_z * weights, -sin_z * weights), axis=0) * SCALE
-        full = np.zeros((4, 128, NZ))
+        one = (parts * weights.reshape(1, 8, 2, 1)).transpose(1, 0, 2, 3) * SCALE
+        full = np.zeros((4, 8, 4, 2, 2, NZ))
         for g in range(4):
-            full[g, g * 32 : (g + 1) * 32] = one
-        hi, lo = split_np(full)
+            full[g, :, g] = one
+        hi, lo = split_np(full.reshape(4, 128, NZ))
         return np.concatenate((hi, hi, lo), axis=1)
 
+    eye = np.eye
+    pick_c = np.einsum(
+        "gG,pP,kK,co->cgpkPKGo", eye(4), eye(2), eye(2), np.ones((8, C))
+    ).reshape(128, 512)
+    pick_o = np.einsum(
+        "hgo,pP,kK,G->hgpkPKGo", eye(C).reshape(4, 8, C).transpose(1, 0, 2), eye(2), eye(2), np.ones(4)
+    ).reshape(128, 512)
     return dict(
         yf=np.stack(split_np(yf), axis=1),
         yi=np.stack(split_np(yi), axis=1),
@@ -75,6 +83,8 @@
         zf=np.concatenate(split_np(zf), axis=1),
         ziw=inverse_z(depth),
         zi1=inverse_z(np.ones((M, 1))),
+        pick_c=pick_c.astype(ml_dtypes.bfloat16),
+        pick_o=pick_o.astype(ml_dtypes.bfloat16),
     )
 
 
@@ -101,8 +111,21 @@
 
 
 def turn(x):
-    real = lax.rem(lane_of(x.shape), 32) < 16
-    return jnp.where(real, pltpu.roll(x, 112, x.ndim - 1), -pltpu.roll(x, 16, x.ndim - 1))
+    real = lax.rem(lane_of(x.shape), 4) < 2
+    return jnp.where(real, pltpu.roll(x, 126, x.ndim - 1), -pltpu.roll(x, 2, x.ndim - 1))
+
+
+def exchange(tiles):
+    tiles = list(tiles)
+    group = lane_of(tiles[0].shape) // 16
+    for step in (1, 2, 4):
+        high = lax.rem(group // step, 2) == 1
+        for t in range(8):
+            if t & step == 0:
+                one, two = tiles[t], tiles[t + step]
+                tiles[t] = jnp.where(high, pltpu.roll(two, 16 * step, 1), one)
+                tiles[t + step] = jnp.where(high, two, pltpu.roll(one, 128 - 16 * step, 1))
+    return tiles
 
 
 def remote(src, dst, send, recv, device):
@@ -196,13 +219,10 @@
 )
 
 INVERSE = dict(
-    ns=pltpu.VMEM((WIDE, 1, 128), F32),
-    nr=pltpu.VMEM((WIDE, 1, 128), F32),
     vs=pltpu.VMEM((WIDE, 8, 128), F32),
     vr=pltpu.VMEM((WIDE, 8, 128), F32),
     as_=pltpu.VMEM((CHUNKS, ROWS, 1024), F32),
     ar=pltpu.VMEM((CHUNKS, NARROW, ROWS, 1024), F32),
-    nsem=pltpu.SemaphoreType.DMA((2,)),
     vsem=pltpu.SemaphoreType.DMA((2,)),
     asem=pltpu.SemaphoreType.DMA((2, CHUNKS)),
 )
@@ -211,10 +231,10 @@
 def depth_forward(field, zf):
     full = dot(field.reshape(YL * C, NZ), zf)
     full = (full[:, :128] + full[:, 128:]).reshape(YL, 4, 8, 128)
-    lane = lane_of((YL, 8, 128))
-    low = jnp.where(lane < 32, full[:, 0], full[:, 1])
-    high = jnp.where(lane < 96, full[:, 2], full[:, 3])
-    return jnp.where(lane < 64, low, high)
+    group = lax.rem(lane_of((YL, 8, 128)) // 4, 4)
+    low = jnp.where(group == 0, full[:, 0], full[:, 1])
+    high = jnp.where(group == 2, full[:, 2], full[:, 3])
+    return jnp.where(group < 2, low, high)
 
 
 class Forward:
@@ -252,24 +272,27 @@
             total = o.yr[q, 0]
             for t in range(1, NARROW):
                 total = total + o.yr[q, t]
+            tiles = exchange([total[:, t * 128 : t * 128 + 128] for t in range(8)])
             for k in range(KY):
-                for c8 in range(8):
-                    o.xs[k * 8 + c8, q * XC : q * XC + XC] = total[
-                        k * XC : k * XC + XC, c8 * 128 : c8 * 128 + 128
-                    ]
+                for t in range(8):
+                    o.xs[k * 8 + t, q * XC : q * XC + XC] = tiles[t][k * XC : k * XC + XC]
         o.xr[self.w] = o.xs[self.w]
         self.x.start()
 
-    def to_owner(self, xf):
+    def modes(self, xf):
         o = self.own
         self.x.arrived()
         cells = o.xr[...].reshape(256, 128)
         hi, lo = halves(jnp.concatenate((cells, turn(cells)), axis=0))
-        o.ms[...] = dot3(xf, hi, lo).reshape(WIDE, 1, 128)
+        return dot3(xf, hi, lo)
+
+    def to_owner(self, modes):
+        o = self.own
+        o.ms[...] = modes.reshape(WIDE, 1, 128)
         o.mr[self.w] = o.ms[self.w]
         self.m.start()
 
-    def modes(self):
+    def owned(self):
         self.m.arrived()
         return self.own.mr[...].reshape(WIDE, 128)
 
@@ -282,23 +305,14 @@
 class Inverse:
     def __init__(self, s, own, n, w):
         self.s, self.own, self.n, self.w = s, own, n, w
-        self.m = Round("wide", WIDE, w, own.ns, own.nr, own.nsem.at[0], own.nsem.at[1])
         self.x = Round("wide", WIDE, w, own.vs, own.vr, own.vsem.at[0], own.vsem.at[1])
 
     def y(self, q):
         o = self.own
         return Round("narrow", NARROW, self.n, o.as_.at[q], o.ar.at[q], o.asem.at[0, q], o.asem.at[1, q])
 
-    def start(self, modes):
+    def to_cells(self, modes, xi):
         o = self.own
-        o.ns[...] = modes.reshape(WIDE, 1, 128)
-        o.nr[self.w] = o.ns[self.w]
-        self.m.start()
-
-    def to_cells(self, xi):
-        o = self.own
-        self.m.arrived()
-        modes = o.nr[...].reshape(WIDE, 128)
         hi, lo = halves(jnp.concatenate((modes, turn(modes)), axis=0))
         o.vs[...] = dot3(xi, hi, lo).reshape(WIDE, 8, 128)
         o.vr[self.w] = o.vs[self.w]
@@ -307,11 +321,12 @@
     def gather(self):
         o = self.own
         self.x.arrived()
+        tiles = [exchange([o.vr[k * 8 + t] for t in range(8)]) for k in range(KY)]
         for q in range(CHUNKS):
             for k in range(KY):
                 for c8 in range(8):
-                    o.as_[q, k * XC : k * XC + XC, c8 * 128 : c8 * 128 + 128] = o.vr[
-                        k * 8 + c8, q * XC : q * XC + XC
+                    o.as_[q, k * XC : k * XC + XC, c8 * 128 : c8 * 128 + 128] = tiles[k][c8][
+                        q * XC : q * XC + XC
                     ]
             o.ar[q, self.n] = o.as_[q]
             self.y(q).start(whole=True)
@@ -339,7 +354,6 @@
             s.field[:, g] = dot(both, zi[g]).reshape(YL, 8, NZ)
 
     def finish(self):
-        self.m.sent()
         self.x.sent()
         loop(CHUNKS, lambda q: self.y(q).sent())
 
@@ -366,78 +380,90 @@
     return h + h * (1.0 - h) * (u * (2.0 * k + (6.0 * k * 0.044715) * square))
 
 
-def by_channel(rows):
-    return jnp.concatenate(
-        [
-            pltpu.roll(rows[k * 8 : k * 8 + 8], (128 - 32 * g) % 128, 1)
-            for k in range(KY)
-            for g in range(4)
-        ],
-        axis=0,
-    )
-
-
-def by_group(pieces):
-    lane = lane_of((8, 128))
-    rows = []
-    for k in range(KY):
-        low = jnp.where(lane < 32, pieces(k, 0), pieces(k, 1))
-        high = jnp.where(lane < 96, pieces(k, 2), pieces(k, 3))
-        rows.append(jnp.where(lane < 64, low, high))
-    return jnp.concatenate(rows, axis=0)
-
-
-def mix_modes(s, modes):
-    def body(kz, columns):
-        for k in range(KY):
-            rows = columns[k * C : k * C + C]
-            real, imag = rows[:, 0:1], rows[:, M : M + 1]
-            w_real, w_imag = s.weight[0, k, kz].astype(F32), s.weight[1, k, kz].astype(F32)
-            s.mt[k, pl.ds(kz, 1), :C] = jnp.sum(real * w_real - imag * w_imag, axis=0, keepdims=True)
-            s.mt[k, pl.ds(kz + M, 1), :C] = jnp.sum(
-                real * w_imag + imag * w_real, axis=0, keepdims=True
-            )
-        return pltpu.roll(columns, 127, 1)
-
-    s.mt[...] = jnp.zeros_like(s.mt)
-    lax.fori_loop(0, M, body, by_channel(modes))
-    turned = s.mt[...].reshape(KY * 2 * M, 128).T
-    return by_group(
-        lambda k, g: pltpu.roll(turned[g * 8 : g * 8 + 8], (128 + 32 * (g - k)) % 128, 1)
-    )
-
-
-def mix_back(s, grads):
-    turned = by_channel(grads).T
-    for k in range(KY):
-        s.gt[k] = pltpu.roll(turned[: 2 * M], (128 - 32 * k) % 128, 1)
-    lane = lane_of((C, 128))
-
-    def body(kz, totals):
-        out = []
-        for k in range(KY):
-            real, imag = s.gt[k, pl.ds(kz, 1), :C], s.gt[k, pl.ds(kz + M, 1), :C]
-            w_real, w_imag = s.weight[0, k, kz].astype(F32), s.weight[1, k, kz].astype(F32)
-            first = jnp.sum(real * w_real + imag * w_imag, axis=1, keepdims=True)
-            second = jnp.sum(imag * w_real - real * w_imag, axis=1, keepdims=True)
-            out.append(jnp.where(lane == kz, first, jnp.where(lane == kz + M, second, totals[k])))
-        return tuple(out)
-
-    totals = lax.fori_loop(0, M, body, tuple(jnp.zeros((C, 128), F32) for _ in range(KY)))
-    return by_group(lambda k, g: pltpu.roll(totals[k][g * 8 : g * 8 + 8], 32 * g, 1))
-
-
-def outer_modes(s, modes):
-    def body(kz, columns):
-        for k in range(KY):
-            rows = columns[k * C : k * C + C]
-            real, imag = rows[:, 0:1], rows[:, M : M + 1]
-            g_real, g_imag = s.gt[k, pl.ds(kz, 1), :C], s.gt[k, pl.ds(kz + M, 1), :C]
-            s.sg[0, k, kz] = real * g_real + imag * g_imag
-            s.sg[1, k, kz] = real * g_imag - imag * g_real
-        return pltpu.roll(columns, 127, 1)
-
-    lax.fori_loop(0, M, body, by_channel(modes))
+def select(rows, pick):
+    hi, lo = halves(rows)
+    return dot(hi, pick) + dot(lo, pick)
+
+
+def gather_back(columns, pick):
+    hi, lo = halves(columns)
+    return dot_t(hi, pick) + dot_t(lo, pick)
+
+
+def part_of(columns, part, k2):
+    at = (2 * part + k2) * 128
+    return columns[:, at : at + 128]
+
+
+def own_channel(rows):
+    row = lax.rem(lax.broadcasted_iota(jnp.int32, rows.shape, 0), 8)
+    return jnp.where(lane_of(rows.shape) // 16 == row, rows, 0.0)
+
+
+def over_rows(rows):
+    lanes = rows.shape[1]
+    return jnp.broadcast_to(rows[:, None], (WIDE, 8, lanes)).reshape(WIDE * 8, lanes)
+
+
+def by_input(modes, pick_c):
+    return select(own_channel(over_rows(modes)), pick_c)
+
+
+def weight_of(wr):
+    def at(part, k2):
+        return wr[:, 2 * part + k2].reshape(WIDE * 8, 128)
+
+    return at
+
+
+def mix_modes(modes, weight, pick_c, pick_o):
+    columns = by_input(modes, pick_c)
+    real, imag = [], []
+    for k2 in range(2):
+        c_real, c_imag = part_of(columns, 0, k2), part_of(columns, 1, k2)
+        w_real, w_imag = weight(0, k2), weight(1, k2)
+        real.append(c_real * w_real - c_imag * w_imag)
+        imag.append(c_real * w_imag + c_imag * w_real)
+    full = jnp.concatenate(real + imag, axis=1).reshape(WIDE, 8, 512)
+    return gather_back(jnp.sum(full, axis=1), pick_o)
+
+
+def mix_back(grads, weight, pick_c, pick_o):
+    columns = over_rows(select(grads, pick_o))
+    real, imag = [], []
+    for k2 in range(2):
+        g_real, g_imag = part_of(columns, 0, k2), part_of(columns, 1, k2)
+        w_real, w_imag = weight(0, k2), weight(1, k2)
+        real.append(g_real * w_real + g_imag * w_imag)
+        imag.append(g_imag * w_real - g_real * w_imag)
+    full = own_channel(gather_back(jnp.concatenate(real + imag, axis=1), pick_c))
+    return jnp.sum(full.reshape(WIDE, 8, 128), axis=1)
+
+
+def outer_modes(s, modes, grads, pick_c, pick_o):
+    first = by_input(modes, pick_c)
+    second = over_rows(select(grads, pick_o))
+    for k2 in range(2):
+        c_real, c_imag = part_of(first, 0, k2), part_of(first, 1, k2)
+        g_real, g_imag = part_of(second, 0, k2), part_of(second, 1, k2)
+        for part, value in enumerate(
+            (c_real * g_real + c_imag * g_imag, c_real * g_imag - c_imag * g_real)
+        ):
+            for g in range(4):
+                moved = pltpu.roll(value, (128 - 32 * g) % 128, 1) if g else value
+                s.sg[part, :, :, k2, g * 8 : g * 8 + 8, :] = moved[:, :C].reshape(KY, 8, 8, C)
+
+
+def pack_weight(s, n, w):
+    def one(k):
+        for part in range(2):
+            for k2 in range(2):
+                full = s.weight[part, k, :, k2].astype(F32)
+                tile = jnp.concatenate([full[:, g * 8 : g * 8 + 8] for g in range(4)], axis=-1)
+                s.ws[pl.ds(pl.multiple_of(k * 8, 8), 8), 2 * part + k2] = tile
+
+    loop(KY, one)
+    s.wr[w] = s.ws[w]
 
 
 def kernel(
@@ -454,6 +480,8 @@
     zf_ref,
     ziw_ref,
     zi1_ref,
+    pick_c_ref,
+    pick_o_ref,
     out_hbm,
     point_grad_ref,
     bias_grad_ref,
@@ -522,24 +550,33 @@
     tall = dot_t(ones, point_ref[...]).astype(BF16)
     s.mix[...] = jnp.where(same, dot_t(tall, ones), 0.0).astype(BF16)
 
-    def blocks(fn):
-        def one(i):
+    def blocks(fn, low, high):
+        def one(i, carry):
             fn(i // 4, pl.ds(pl.multiple_of(lax.rem(i, 4) * 8, 8), 8))
-
-        loop(4 * XL, one)
+            return carry
+
+        lax.fori_loop(low, high, one, 0)
 
     def mix_block(x, ys):
         point = dot(s.mix[...], s.act[x, ys].reshape(256, NZ)) + bias_rows
         s.point[x, ys] = point.reshape(8, C, NZ)
 
-    blocks(mix_block)
+    weight_copy.wait()
+    pack_weight(s, n, w)
+    weight_round = Round("wide", WIDE, w, s.ws, s.wr, s.wsem.at[0], s.wsem.at[1])
+    weight_round.start()
+    pick_c, pick_o = pick_c_ref[...], pick_o_ref[...]
+    weight = weight_of(s.wr)
+    blocks(mix_block, 0, 20)
     ahead.sum_chunks()
-    ahead.to_owner(xf_ref)
-    weight_copy.wait()
-    mixed_in.start(mix_modes(s, ahead.modes()))
+    blocks(mix_block, 20, 26)
+    weight_round.arrived()
+    coeffs = ahead.modes(xf_ref)
+    mixed_in.to_cells(mix_modes(coeffs, weight, pick_c, pick_o), xi_ref)
+    ahead.to_owner(coeffs)
     s.bs[...] = jnp.zeros_like(s.bs)
     s.pg[...] = jnp.zeros_like(s.pg)
-    mixed_in.to_cells(xi_ref)
+    blocks(mix_block, 26, 4 * XL)
     mixed_in.gather()
 
     def middle_chunk(q):
@@ -572,29 +609,30 @@
         s.pg[...] += dot_t(s.act[x, ys].reshape(256, NZ), pre)
         s.point[x, ys] = dot(s.mix_back[...], pre).reshape(8, C, NZ)
 
-    blocks(back_block)
+    blocks(back_block, 0, 8)
+    grad.sum_chunks()
+    blocks(back_block, 8, 20)
+    rows = grad.modes(xf_ref)
+    first = lax.rem(w, 8) == 0
+    grads = rows * jnp.where((lax.rem(lane_of(rows.shape), 2) == 0) & first, 1.0, 2.0)
+    back_in.to_cells(mix_back(grads, weight, pick_c, pick_o), xi_ref)
+    grad.to_owner(grads)
+    blocks(back_block, 20, 4 * XL)
     s.ps[0:8] = fold_point(s.pg[...])
     s.ps[8:16] = s.bs[...]
     s.pr[n] = s.ps[...]
-    grad.sum_chunks()
+    back_in.gather()
     narrow_sum = Round("narrow", NARROW, n, s.ps, s.pr, s.psem.at[0], s.psem.at[1])
     narrow_sum.start(whole=True)
-    grad.to_owner(xf_ref)
+    outer_modes(s, ahead.owned(), grad.owned(), pick_c, pick_o)
+    sg_copy.start()
     narrow_sum.arrived()
     total = s.pr[0]
     for t in range(1, NARROW):
         total = total + s.pr[t]
     s.ts[...] = total
     s.tr[w] = total
-    rows = grad.modes()
-    depth_weight = jnp.where(lax.rem(lane_of(rows.shape), 16) == 0, 1.0, 2.0)
-    grads = rows * depth_weight
-    back_in.start(mix_back(s, grads))
-    outer_modes(s, ahead.own.mr[...].reshape(WIDE, 128))
-    sg_copy.start()
-    back_in.to_cells(xi_ref)
     wide_sum = Round("wide", WIDE, w, s.ts, s.tr, s.tsem.at[0], s.tsem.at[1])
-    back_in.gather()
     wide_sum.start(whole=True)
 
     def last_chunk(q):
@@ -624,12 +662,13 @@
     row, lane = lax.broadcasted_iota(jnp.int32, (8, C), 0), lane_of((8, C))
     bias_grad = jnp.zeros((8, C), F32)
     for g in range(4):
-        bias_grad = jnp.where(lane == g * 8 + row, total[8:16, g * 32 : g * 32 + 1], bias_grad)
+        bias_grad = jnp.where(lane == g * 8 + row, total[8:16, g * 4 : g * 4 + 1], bias_grad)
     bias_grad_ref[...] = SCALE * jnp.sum(bias_grad, axis=0, keepdims=True)
     for part in (ahead, grad, mixed_in, back_in):
         part.finish()
     narrow_sum.sent()
     wide_sum.sent()
+    weight_round.sent()
     sg_copy.wait()
     loop(XL, lambda x: out_copy(x).wait())
 
@@ -656,10 +695,10 @@
         yi=pltpu.VMEM((2, 32 * XC, 64 * XC), BF16),
         mix=pltpu.VMEM((256, 256), BF16),
         mix_back=pltpu.VMEM((256, 256), BF16),
-        weight=pltpu.VMEM((2, KY, M, C, C), BF16),
-        sg=pltpu.VMEM((2, KY, M, C, C), F32),
-        mt=pltpu.VMEM((KY, 2 * M, 128), F32),
-        gt=pltpu.VMEM((KY, 2 * M, 128), F32),
+        weight=pltpu.VMEM((2, KY, 8, 2, C, C), BF16),
+        sg=pltpu.VMEM((2, KY, 8, 2, C, C), F32),
+        ws=pltpu.VMEM((WIDE, 4, 8, 128), F32),
+        wr=pltpu.VMEM((WIDE, 4, 8, 128), F32),
         pg=pltpu.VMEM((256, 256), F32),
         bs=pltpu.VMEM((8, 128), F32),
         ps=pltpu.VMEM((16, 128), F32),
@@ -670,6 +709,7 @@
         cot_sem=pltpu.SemaphoreType.DMA((XL,)),
         out_sem=pltpu.SemaphoreType.DMA((XL,)),
         table_sem=pltpu.SemaphoreType.DMA((4,)),
+        wsem=pltpu.SemaphoreType.DMA((2,)),
         psem=pltpu.SemaphoreType.DMA((2,)),
         tsem=pltpu.SemaphoreType.DMA((2,)),
     )
@@ -678,13 +718,13 @@
     input_grad, point_grad, bias_grad, spectral_grad = pl.pallas_call(
         functools.partial(kernel, tuple(scratch)),
         name="layer_backward",
-        in_specs=[HB, HB, VM, VM, HB, HB, HB, VM, VM, VM, VM, VM],
+        in_specs=[HB, HB, VM, VM, HB, HB, HB, VM, VM, VM, VM, VM, VM, VM],
         out_specs=[HB, VM, VM, HB],
         out_shape=[
             jax.ShapeDtypeStruct(FIELD, BF16),
             jax.ShapeDtypeStruct((C, C), F32),
             jax.ShapeDtypeStruct((1, C), F32),
-            jax.ShapeDtypeStruct((2, 1, KY, M, C, C), F32),
+            jax.ShapeDtypeStruct((2, 1, KY, 8, 2, C, C), F32),
         ],
         scratch_shapes=tuple(scratch.values()),
         compiler_params=pltpu.CompilerParams(
@@ -695,10 +735,11 @@
         cotangent,
         point_weight,
         bias[None],
-        spectral_weight,
-        *(tabs[name] for name in ("yf", "yi", "xf", "xi", "zf", "ziw", "zi1")),
+        spectral_weight.reshape(2, 1, KY, 8, 2, C, C),
+        *(tabs[name] for name in ("yf", "yi", "xf", "xi", "zf", "ziw", "zi1", "pick_c", "pick_o")),
     )
 
+    spectral_grad = spectral_grad.reshape(2, 1, KY, M, C, C)
     return (input_grad, point_grad, bias_grad.reshape(C), spectral_grad)
 
 

time: 137 us -> 121 us (0.88)
  Pallas kernels: 129 us -> 113 us
    pallas_call x1, Pallas kernels: 129 us -> 113 us  [local(): pl.pallas_call(functools.partial(kernel, tuple(scratch)), name='layer_bac...]
where the time goes in v4:
time: 121 us
  Pallas kernels  113 us (93%)
  local copies, waits for them, and re-layouts  7.24 us (6%)
    pallas_call x1, Pallas kernels, local(): pl.pallas_call(functools.partial(kernel, tuple(scratch)), name='layer_bac...  113 us
    unnamed x10, local copies, waits for them, and re-layouts  7.24 us

profile of v4, /device:TPU:1, one launch (start us, length us, event | category | flops | bytes accessed | tf_op | source)
XLA Modules:
  0.0 121.2 jit_solution(6325532054212577516)
XLA Ops:
  0.6 113.3 %layer_backward.1 = (bf16[8,32,32,256]{3,2,1,0:T(8,128)(2,1)}, f32[32,32]{1,0:T(8,128)}, f32[1,32]{1,0:T(1,128)}, f32[2,1,4,8,2,32,32]{6,5,4,3,2,1,0:T(8,128)}) custom-call(bf16[8,32,32,256]{3,2,1,0:T(8,128)(2,1)} %act_hbm.1, bf16[8,32,32,256]{3,2,1,0:T(8,128)(2,1)} %cot_hbm.1, bf16[32,32]{1,0:T(8,128)(2,1)} %point_ref.1, f32[1,32]{1,0:T(1,128)} %bitcast.8, ...), custom_call_target="tpu_custom_call" | custom-call | tf_op jit(solution)/shard_map/layer_backward/pallas_call | solution.py:718
  113.9 0.0 copy-start.1
  113.9 0.0 copy-start.2
  113.9 0.0 copy-start
  113.9 4.8 %copy.23 = bf16[8,32,32,256]{3,2,1,0:T(8,128)(2,1)} copy(bf16[8,32,32,256]{3,2,1,0:T(8,128)(2,1)} %get-tuple-element.20) | data formatting | bytes 8388608
  118.7 0.0 copy-done.1
  118.7 0.6 copy.24
  119.3 0.0 copy-done.2
  119.3 0.5 copy.25
  119.8 0.0 copy-done
  119.8 1.3 %copy.26 = f32[2,1,4,16,32,32]{5,4,3,2,1,0:T(8,128)} copy(f32[2,1,4,16,32,32]{5,4,3,2,1,0:T(8,128)S(1)} %bitcast.6) | data formatting | bytes 1048576
Async XLA Ops:
  113.9 4.8 %copy-start.1 = (f32[32,32]{1,0:T(8,128)S(1)}, f32[32,32]{1,0:T(8,128)}, u32[]{:S(2)}) copy-start(f32[32,32]{1,0:T(8,128)} %get-tuple-element.21) | copy-start | bytes 12292
  113.9 5.4 %copy-start.2 = (f32[1,32]{1,0:T(1,128)S(1)}, f32[1,32]{1,0:T(1,128)}, u32[]{:S(2)}) copy-start(f32[1,32]{1,0:T(1,128)} %get-tuple-element.10) | copy-start | bytes 388
  113.9 5.9 %copy-start = (f32[2,1,4,8,2,32,32]{6,5,4,3,2,1,0:T(8,128)S(1)}, f32[2,1,4,8,2,32,32]{6,5,4,3,2,1,0:T(8,128)}, u32[]{:S(2)}) copy-start(f32[2,1,4,8,2,32,32]{6,5,4,3,2,1,0:T(8,128)} %get-tuple-element.11) | copy-start | bytes 1572868

commit v5 on v4

--- a/solution.py
+++ b/solution.py
@@ -147,6 +147,19 @@
     lax.fori_loop(1, size, body, 0)
 
 
+def far_first(me, size, fn):
+    x, z, core = me // 16, lax.rem(me // 2, 8), lax.rem(me, 2)
+
+    def body(j, carry):
+        i, sub = j // 4, lax.rem(j, 4)
+        dz = 4 + (1 - 2 * lax.rem(i, 2)) * ((i + 1) // 2)
+        dx, dcore = 1 - sub // 2, 1 - lax.rem(sub, 2)
+        fn(lax.rem(x + dx, 2) * 16 + lax.rem(z + dz, 8) * 2 + lax.rem(core + dcore, 2))
+        return carry
+
+    lax.fori_loop(0, size - 1, body, 0)
+
+
 def greet(n, w):
     barrier = pltpu.get_barrier_semaphore()
 
@@ -184,6 +197,8 @@
         self.src, self.dst, self.send, self.recv = src, dst, send, recv
 
     def start(self, whole=False):
+        order = far_first if self.size == WIDE else others
+
         def one(t):
             remote(
                 self.src if whole else self.src.at[t],
@@ -193,7 +208,7 @@
                 {self.axis: t},
             ).start()
 
-        others(self.me, self.size, one)
+        order(self.me, self.size, one)
 
     def all_of(self):
         part = self.dst.at[pl.ds(0, self.size - 1)]
@@ -440,7 +455,7 @@
     return jnp.sum(full.reshape(WIDE, 8, 128), axis=1)
 
 
-def outer_modes(s, modes, grads, pick_c, pick_o):
+def outer_modes(sg_ref, modes, grads, pick_c, pick_o):
     first = by_input(modes, pick_c)
     second = over_rows(select(grads, pick_o))
     for k2 in range(2):
@@ -451,7 +466,7 @@
         ):
             for g in range(4):
                 moved = pltpu.roll(value, (128 - 32 * g) % 128, 1) if g else value
-                s.sg[part, :, :, k2, g * 8 : g * 8 + 8, :] = moved[:, :C].reshape(KY, 8, 8, C)
+                sg_ref[part, 0, :, :, k2, g * 8 : g * 8 + 8, :] = moved[:, :C].reshape(KY, 8, 8, C)
 
 
 def pack_weight(s, n, w):
@@ -482,10 +497,10 @@
     zi1_ref,
     pick_c_ref,
     pick_o_ref,
-    out_hbm,
+    out_ref,
     point_grad_ref,
     bias_grad_ref,
-    sg_hbm,
+    sg_ref,
     *refs,
 ):
     s = Names(names, refs)
@@ -505,22 +520,21 @@
 
     def cot_copy(x):
         return pltpu.make_async_copy(cot_hbm.at[x], s.cot.at[x], s.cot_sem.at[x])
-
-    def out_copy(x):
-        return pltpu.make_async_copy(s.out.at[x], out_hbm.at[x], s.out_sem.at[x])
 
     table_in = [
         pltpu.make_async_copy(yf_hbm.at[n], s.yf, s.table_sem.at[0]),
         pltpu.make_async_copy(yi_hbm.at[n], s.yi, s.table_sem.at[1]),
     ]
     weight_copy = pltpu.make_async_copy(weight_hbm.at[:, 0], s.weight, s.table_sem.at[2])
-    sg_copy = pltpu.make_async_copy(s.sg, sg_hbm.at[:, 0], s.table_sem.at[3])
+    weight_copy.start()
     barrier = greet(n, w)
-    loop(XL, lambda x: act_copy(x).start())
     for copy in table_in:
         copy.start()
-    weight_copy.start()
+    loop(XL, lambda x: act_copy(x).start())
     loop(XL, lambda x: cot_copy(x).start())
+    weight_round = Round("wide", WIDE, w, s.ws, s.wr, s.wsem.at[0], s.wsem.at[1])
+    weight_copy.wait()
+    pack_weight(s, n, w)
     for copy in table_in:
         copy.wait()
 
@@ -537,6 +551,10 @@
             greeted(barrier)
 
         ahead.send_chunk(q)
+
+        @pl.when(q == 0)
+        def _():
+            weight_round.start()
 
     loop(CHUNKS, forward_chunk)
 
@@ -561,10 +579,6 @@
         point = dot(s.mix[...], s.act[x, ys].reshape(256, NZ)) + bias_rows
         s.point[x, ys] = point.reshape(8, C, NZ)
 
-    weight_copy.wait()
-    pack_weight(s, n, w)
-    weight_round = Round("wide", WIDE, w, s.ws, s.wr, s.wsem.at[0], s.wsem.at[1])
-    weight_round.start()
     pick_c, pick_o = pick_c_ref[...], pick_o_ref[...]
     weight = weight_of(s.wr)
     blocks(mix_block, 0, 20)
@@ -621,11 +635,10 @@
     s.ps[0:8] = fold_point(s.pg[...])
     s.ps[8:16] = s.bs[...]
     s.pr[n] = s.ps[...]
-    back_in.gather()
     narrow_sum = Round("narrow", NARROW, n, s.ps, s.pr, s.psem.at[0], s.psem.at[1])
     narrow_sum.start(whole=True)
-    outer_modes(s, ahead.owned(), grad.owned(), pick_c, pick_o)
-    sg_copy.start()
+    back_in.gather()
+    outer_modes(sg_ref, ahead.owned(), grad.owned(), pick_c, pick_o)
     narrow_sum.arrived()
     total = s.pr[0]
     for t in range(1, NARROW):
@@ -645,10 +658,9 @@
             def block(b):
                 ys = pl.ds(pl.multiple_of(b * 8, 8), 8)
                 out = s.field[ys].reshape(256, NZ) + s.point[x, ys].reshape(256, NZ)
-                s.out[x, ys] = out.astype(BF16).reshape(8, C, NZ)
+                out_ref[x, ys] = out.astype(BF16).reshape(8, C, NZ)
 
             loop(4, block)
-            out_copy(x).start()
 
         loop(XC, row)
 
@@ -669,8 +681,32 @@
     narrow_sum.sent()
     wide_sum.sent()
     weight_round.sent()
-    sg_copy.wait()
-    loop(XL, lambda x: out_copy(x).wait())
+
+
+def write_kernel(*refs):
+    sources, targets, sems = refs[:4], refs[4:8], refs[8]
+    copies = [
+        pltpu.make_async_copy(sources[0].at[x], targets[0].at[x], sems.at[x]) for x in range(XL)
+    ] + [
+        pltpu.make_async_copy(source, target, sems.at[XL + i])
+        for i, (source, target) in enumerate(zip(sources[1:], targets[1:]))
+    ]
+    for copy in copies:
+        copy.start()
+    for copy in copies:
+        copy.wait()
+
+
+def write_out(*arrays):
+    return pl.pallas_call(
+        write_kernel,
+        name="write_results",
+        in_specs=[VM] * 4,
+        out_specs=[HB] * 4,
+        out_shape=[jax.ShapeDtypeStruct(a.shape, a.dtype) for a in arrays],
+        scratch_shapes=[pltpu.SemaphoreType.DMA((XL + 3,))],
+        compiler_params=pltpu.CompilerParams(vmem_limit_bytes=1024 * 1024),
+    )(*arrays)
 
 
 VM = pl.BlockSpec(memory_space=pltpu.VMEM)
@@ -684,7 +720,6 @@
         act=pltpu.VMEM(FIELD, BF16),
         cot=pltpu.VMEM(FIELD, BF16),
         pre=pltpu.VMEM(FIELD, BF16),
-        out=pltpu.VMEM(FIELD, BF16),
         point=pltpu.VMEM(FIELD, F32),
         field=pltpu.VMEM((YL, 4, 8, NZ), F32),
         d=pltpu.VMEM((256, 128), F32),
@@ -696,7 +731,6 @@
         mix=pltpu.VMEM((256, 256), BF16),
         mix_back=pltpu.VMEM((256, 256), BF16),
         weight=pltpu.VMEM((2, KY, 8, 2, C, C), BF16),
-        sg=pltpu.VMEM((2, KY, 8, 2, C, C), F32),
         ws=pltpu.VMEM((WIDE, 4, 8, 128), F32),
         wr=pltpu.VMEM((WIDE, 4, 8, 128), F32),
         pg=pltpu.VMEM((256, 256), F32),
@@ -707,7 +741,6 @@
         tr=pltpu.VMEM((WIDE, 16, 128), F32),
         act_sem=pltpu.SemaphoreType.DMA((XL,)),
         cot_sem=pltpu.SemaphoreType.DMA((XL,)),
-        out_sem=pltpu.SemaphoreType.DMA((XL,)),
         table_sem=pltpu.SemaphoreType.DMA((4,)),
         wsem=pltpu.SemaphoreType.DMA((2,)),
         psem=pltpu.SemaphoreType.DMA((2,)),
@@ -719,16 +752,16 @@
         functools.partial(kernel, tuple(scratch)),
         name="layer_backward",
         in_specs=[HB, HB, VM, VM, HB, HB, HB, VM, VM, VM, VM, VM, VM, VM],
-        out_specs=[HB, VM, VM, HB],
+        out_specs=[VM, VM, VM, VM],
         out_shape=[
-            jax.ShapeDtypeStruct(FIELD, BF16),
-            jax.ShapeDtypeStruct((C, C), F32),
-            jax.ShapeDtypeStruct((1, C), F32),
-            jax.ShapeDtypeStruct((2, 1, KY, 8, 2, C, C), F32),
+            pltpu.VMEM(FIELD, BF16),
+            pltpu.VMEM((C, C), F32),
+            pltpu.VMEM((1, C), F32),
+            pltpu.VMEM((2, 1, KY, 8, 2, C, C), F32),
         ],
         scratch_shapes=tuple(scratch.values()),
         compiler_params=pltpu.CompilerParams(
-            collective_id=0, has_side_effects=True, vmem_limit_bytes=56 * 1024 * 1024
+            collective_id=0, has_side_effects=True, vmem_limit_bytes=48 * 1024 * 1024
         ),
     )(
         activations,
@@ -739,6 +772,9 @@
         *(tabs[name] for name in ("yf", "yi", "xf", "xi", "zf", "ziw", "zi1", "pick_c", "pick_o")),
     )
 
+    input_grad, point_grad, bias_grad, spectral_grad = write_out(
+        input_grad, point_grad, bias_grad, spectral_grad
+    )
     spectral_grad = spectral_grad.reshape(2, 1, KY, M, C, C)
     return (input_grad, point_grad, bias_grad.reshape(C), spectral_grad)
 

time: 121 us -> 109 us (0.901)
  local copies, waits for them, and re-layouts: 7.24 us -> 0 us
  Pallas kernels: 113 us -> 108 us
    pallas_call x1, Pallas kernels: 113 us -> 105 us  [local(): pl.pallas_call(functools.partial(kernel, tuple(scratch)), name='layer_bac...]
    unnamed x10 -> x0, local copies, waits for them, and re-layouts: 7.24 us -> none
    pallas_call x0 -> x1, Pallas kernels: none -> 2.81 us  [write_out(): pl.pallas_call(write_kernel, name='write_results', in_specs=[VM] * 4, out...]
where the time goes in v5:
time: 109 us
  Pallas kernels  108 us (99%)
    pallas_call x1, Pallas kernels, local(): pl.pallas_call(functools.partial(kernel, tuple(scratch)), name='layer_bac...  105 us
    pallas_call x1, Pallas kernels, write_out(): pl.pallas_call(write_kernel, name='write_results', in_specs=[VM] * 4, out...  2.81 us

profile of v5, /device:TPU:1, one launch (start us, length us, event | category | flops | bytes accessed | tf_op | source)
XLA Modules:
  0.0 108.8 jit_solution(7654718942957079579)
XLA Ops:
  0.6 105.3 %layer_backward.1 = (bf16[8,32,32,256]{3,2,1,0:T(8,128)(2,1)S(1)}, f32[32,32]{1,0:T(8,128)S(1)}, f32[1,32]{1,0:T(1,128)S(1)}, f32[2,1,4,8,2,32,32]{6,5,4,3,2,1,0:T(8,128)S(1)}) custom-call(bf16[8,32,32,256]{3,2,1,0:T(8,128)(2,1)} %act_hbm.1, bf16[8,32,32,256]{3,2,1,0:T(8,128)(2,1)} %cot_hbm.1, bf16[32,32]{1,0:T(8,128)(2,1)} %point_ref.1, f32[1,32]{1,0:T(1,128)} %bitcast.7, ...), custom_call_target="tpu_custom_call" | custom-call | tf_op jit(solution)/shard_map/layer_backward/pallas_call | solution.py:751
  106.0 2.8 %write_results.1 = (bf16[8,32,32,256]{3,2,1,0:T(8,128)(2,1)}, f32[32,32]{1,0:T(8,128)}, f32[1,32]{1,0:T(1,128)}, f32[2,1,4,8,2,32,32]{6,5,4,3,2,1,0:T(8,128)}) custom-call(bf16[8,32,32,256]{3,2,1,0:T(8,128)(2,1)S(1)} %get-tuple-element.12.refs_0_, f32[32,32]{1,0:T(8,128)S(1)} %get-tuple-element.13.refs_1_, f32[1,32]{1,0:T(1,128)S(1)} %get-tuple-element.14.refs_2_, ...), custom_call_target="tpu_custom_call" | custom-call | tf_op jit(solution)/shard_map/write_results/pallas_call | solution.py:701

commit v6 on v5

--- a/solution.py
+++ b/solution.py
@@ -139,22 +139,18 @@
     )
 
 
-def others(me, size, fn):
-    def body(k, carry):
-        fn(lax.rem(me + k, size))
-        return carry
-
-    lax.fori_loop(1, size, body, 0)
-
-
 def far_first(me, size, fn):
-    x, z, core = me // 16, lax.rem(me // 2, 8), lax.rem(me, 2)
+    fast = 4 if size == WIDE else 2
+    ring = 8 if size == WIDE else 4
+    x, z, last = me // 16, lax.rem(me // 2, ring), lax.rem(me, 2)
 
     def body(j, carry):
-        i, sub = j // 4, lax.rem(j, 4)
-        dz = 4 + (1 - 2 * lax.rem(i, 2)) * ((i + 1) // 2)
-        dx, dcore = 1 - sub // 2, 1 - lax.rem(sub, 2)
-        fn(lax.rem(x + dx, 2) * 16 + lax.rem(z + dz, 8) * 2 + lax.rem(core + dcore, 2))
+        i, sub = j // fast, lax.rem(j, fast)
+        dz = ring // 2 + (1 - 2 * lax.rem(i, 2)) * ((i + 1) // 2)
+        to = lax.rem(z + dz, ring) * 2 + lax.rem(last + 1 - lax.rem(sub, 2), 2)
+        if size == WIDE:
+            to = to + lax.rem(x + 1 - sub // 2, 2) * 16
+        fn(to)
         return carry
 
     lax.fori_loop(0, size - 1, body, 0)
@@ -168,8 +164,8 @@
             barrier, inc=1, device_id={axis: t}, device_id_type=pl.DeviceIdType.MESH
         )
 
-    others(n, NARROW, signal("narrow"))
-    others(w, WIDE, signal("wide"))
+    far_first(w, WIDE, signal("wide"))
+    far_first(n, NARROW, signal("narrow"))
     return barrier
 
 
@@ -197,8 +193,6 @@
         self.src, self.dst, self.send, self.recv = src, dst, send, recv
 
     def start(self, whole=False):
-        order = far_first if self.size == WIDE else others
-
         def one(t):
             remote(
                 self.src if whole else self.src.at[t],
@@ -208,7 +202,7 @@
                 {self.axis: t},
             ).start()
 
-        order(self.me, self.size, one)
+        far_first(self.me, self.size, one)
 
     def all_of(self):
         part = self.dst.at[pl.ds(0, self.size - 1)]
@@ -490,13 +484,13 @@
     weight_hbm,
     yf_hbm,
     yi_hbm,
-    xf_ref,
-    xi_ref,
+    xf_hbm,
+    xi_hbm,
     zf_ref,
-    ziw_ref,
-    zi1_ref,
-    pick_c_ref,
-    pick_o_ref,
+    ziw_hbm,
+    zi1_hbm,
+    pick_c_hbm,
+    pick_o_hbm,
     out_ref,
     point_grad_ref,
     bias_grad_ref,
@@ -521,6 +515,19 @@
     def cot_copy(x):
         return pltpu.make_async_copy(cot_hbm.at[x], s.cot.at[x], s.cot_sem.at[x])
 
+    later = [
+        pltpu.make_async_copy(source, target, s.later_sem.at[i])
+        for i, (source, target) in enumerate(
+            (
+                (xf_hbm, s.xf),
+                (xi_hbm, s.xi),
+                (pick_c_hbm, s.pick_c),
+                (pick_o_hbm, s.pick_o),
+                (ziw_hbm, s.ziw),
+                (zi1_hbm, s.zi1),
+            )
+        )
+    ]
     table_in = [
         pltpu.make_async_copy(yf_hbm.at[n], s.yf, s.table_sem.at[0]),
         pltpu.make_async_copy(yi_hbm.at[n], s.yi, s.table_sem.at[1]),
@@ -531,6 +538,8 @@
     for copy in table_in:
         copy.start()
     loop(XL, lambda x: act_copy(x).start())
+    for copy in later:
+        copy.start()
     loop(XL, lambda x: cot_copy(x).start())
     weight_round = Round("wide", WIDE, w, s.ws, s.wr, s.wsem.at[0], s.wsem.at[1])
     weight_copy.wait()
@@ -579,7 +588,10 @@
         point = dot(s.mix[...], s.act[x, ys].reshape(256, NZ)) + bias_rows
         s.point[x, ys] = point.reshape(8, C, NZ)
 
-    pick_c, pick_o = pick_c_ref[...], pick_o_ref[...]
+    for copy in later:
+        copy.wait()
+    xf_ref, xi_ref, ziw_ref, zi1_ref = s.xf, s.xi, s.ziw, s.zi1
+    pick_c, pick_o = s.pick_c[...], s.pick_o[...]
     weight = weight_of(s.wr)
     blocks(mix_block, 0, 20)
     ahead.sum_chunks()
@@ -648,6 +660,19 @@
     wide_sum = Round("wide", WIDE, w, s.ts, s.tr, s.tsem.at[0], s.tsem.at[1])
     wide_sum.start(whole=True)
 
+    def pointwise_totals():
+        wide_sum.arrived()
+        total = s.tr[0]
+        for t in range(1, WIDE):
+            total = total + s.tr[t]
+        for g in range(4):
+            point_grad_ref[g * 8 : g * 8 + 8] = SCALE * total[0:8, g * 32 : g * 32 + C]
+        row, lane = lax.broadcasted_iota(jnp.int32, (8, C), 0), lane_of((8, C))
+        bias_grad = jnp.zeros((8, C), F32)
+        for g in range(4):
+            bias_grad = jnp.where(lane == g * 8 + row, total[8:16, g * 4 : g * 4 + 1], bias_grad)
+        bias_grad_ref[...] = SCALE * jnp.sum(bias_grad, axis=0, keepdims=True)
+
     def last_chunk(q):
         back_in.chunk(q)
 
@@ -665,17 +690,7 @@
         loop(XC, row)
 
     loop(CHUNKS, last_chunk)
-    wide_sum.arrived()
-    total = s.tr[0]
-    for t in range(1, WIDE):
-        total = total + s.tr[t]
-    for g in range(4):
-        point_grad_ref[g * 8 : g * 8 + 8] = SCALE * total[0:8, g * 32 : g * 32 + C]
-    row, lane = lax.broadcasted_iota(jnp.int32, (8, C), 0), lane_of((8, C))
-    bias_grad = jnp.zeros((8, C), F32)
-    for g in range(4):
-        bias_grad = jnp.where(lane == g * 8 + row, total[8:16, g * 4 : g * 4 + 1], bias_grad)
-    bias_grad_ref[...] = SCALE * jnp.sum(bias_grad, axis=0, keepdims=True)
+    pointwise_totals()
     for part in (ahead, grad, mixed_in, back_in):
         part.finish()
     narrow_sum.sent()
@@ -728,6 +743,13 @@
         s=pltpu.VMEM((XC * 256, 128), F32),
         yf=pltpu.VMEM((2, 32 * XC, 64 * XC), BF16),
         yi=pltpu.VMEM((2, 32 * XC, 64 * XC), BF16),
+        xf=pltpu.VMEM((2, 32, 512), BF16),
+        xi=pltpu.VMEM((2, 256, 64), BF16),
+        pick_c=pltpu.VMEM((128, 512), BF16),
+        pick_o=pltpu.VMEM((128, 512), BF16),
+        ziw=pltpu.VMEM((4, 384, NZ), BF16),
+        zi1=pltpu.VMEM((4, 384, NZ), BF16),
+        later_sem=pltpu.SemaphoreType.DMA((6,)),
         mix=pltpu.VMEM((256, 256), BF16),
         mix_back=pltpu.VMEM((256, 256), BF16),
         weight=pltpu.VMEM((2, KY, 8, 2, C, C), BF16),
@@ -751,7 +773,7 @@
     input_grad, point_grad, bias_grad, spectral_grad = pl.pallas_call(
         functools.partial(kernel, tuple(scratch)),
         name="layer_backward",
-        in_specs=[HB, HB, VM, VM, HB, HB, HB, VM, VM, VM, VM, VM, VM, VM],
+        in_specs=[HB, HB, VM, VM, HB, HB, HB, HB, HB, VM, HB, HB, HB, HB],
         out_specs=[VM, VM, VM, VM],
         out_shape=[
             pltpu.VMEM(FIELD, BF16),

time: 109 us -> 108 us (level)
  no operation moved by 1% of the time
where the time goes in v6:
time: 108 us
  Pallas kernels  108 us (100%)
    pallas_call x1, Pallas kernels, local(): pl.pallas_call(functools.partial(kernel, tuple(scratch)), name='layer_bac...  105 us
    pallas_call x1, Pallas kernels, write_out(): pl.pallas_call(write_kernel, name='write_results', in_specs=[VM] * 4, out...  2.81 us

profile of v6, /device:TPU:1, one launch (start us, length us, event | category | flops | bytes accessed | tf_op | source)
XLA Modules:
  0.0 108.3 jit_solution(8672456186758469494)
XLA Ops:
  0.6 104.9 %layer_backward.1 = (bf16[8,32,32,256]{3,2,1,0:T(8,128)(2,1)S(1)}, f32[32,32]{1,0:T(8,128)S(1)}, f32[1,32]{1,0:T(1,128)S(1)}, f32[2,1,4,8,2,32,32]{6,5,4,3,2,1,0:T(8,128)S(1)}) custom-call(bf16[8,32,32,256]{3,2,1,0:T(8,128)(2,1)} %act_hbm.1, bf16[8,32,32,256]{3,2,1,0:T(8,128)(2,1)} %cot_hbm.1, bf16[32,32]{1,0:T(8,128)(2,1)} %point_ref.1, f32[1,32]{1,0:T(1,128)} %bitcast.7, ...), custom_call_target="tpu_custom_call" | custom-call | tf_op jit(solution)/shard_map/layer_backward/pallas_call | solution.py:773
  105.5 2.8 %write_results.1 = (bf16[8,32,32,256]{3,2,1,0:T(8,128)(2,1)}, f32[32,32]{1,0:T(8,128)}, f32[1,32]{1,0:T(1,128)}, f32[2,1,4,8,2,32,32]{6,5,4,3,2,1,0:T(8,128)}) custom-call(bf16[8,32,32,256]{3,2,1,0:T(8,128)(2,1)S(1)} %get-tuple-element.12.refs_0_, f32[32,32]{1,0:T(8,128)S(1)} %get-tuple-element.13.refs_1_, f32[1,32]{1,0:T(1,128)S(1)} %get-tuple-element.14.refs_2_, ...), custom_call_target="tpu_custom_call" | custom-call | tf_op jit(solution)/shard_map/write_results/pallas_call | solution.py:716
